TPU v7x, 32 devices: a whole 2x2x4 slice. The times are simulated.
32 devices in a mesh: dp: 8 (over y, x, core), tensor: 4 (over z).
Axes of the slice: x: 2, y: 2, z: 4, core: 2. Of those that a mesh axis runs over, the one named last changes fastest.
Arguments:
- tokens: bfloat16 [4096, 1536], P(('dp', 'tensor')), may hold values from -6 to 6
- grad_out: bfloat16 [4096, 1536], P(('dp', 'tensor')), may hold values from -6 to 6
- attn_gain: float32 [1536], replicated, may hold values from 0.1 to 1.9
- w_query: bfloat16 [1536, 1536], P('dp', 'tensor'), may hold values from -0.15625 to 0.15625
- b_query: float32 [1536], replicated, may hold values from -2 to 2
- w_key: bfloat16 [1536, 256], P('dp'), may hold values from -0.15625 to 0.15625
- b_key: float32 [256], replicated, may hold values from -2 to 2
- w_value: bfloat16 [1536, 256], P('dp'), may hold values from -0.15625 to 0.15625
- b_value: float32 [256], replicated, may hold values from -1.5 to 1.5
- w_out: bfloat16 [1536, 1536], P('dp', 'tensor'), may hold values from -0.3125 to 0.3125
- mlp_gain: float32 [1536], replicated, may hold values from 0.1 to 1.9
- w_gate: bfloat16 [1536, 8960], P('dp', 'tensor'), may hold values from -0.15625 to 0.15625
- w_up: bfloat16 [1536, 8960], P('dp', 'tensor'), may hold values from -0.15625 to 0.15625
- w_down: bfloat16 [1536, 8960], P('dp', 'tensor'), may hold values from -0.125 to 0.125
Outputs:
- out: float32 [4096, 1536], P(('dp', 'tensor'))
- grad_in: float32 [4096, 1536], P(('dp', 'tensor'))
- grad_attn_gain: float32 [1536], P(('dp', 'tensor'))
- grad_w_query: float32 [1536, 1536], P('dp', 'tensor')
- grad_b_query: float32 [1536], P(('dp', 'tensor'))
- grad_w_key: float32 [1536, 256], P(('dp', 'tensor'))
- grad_b_key: float32 [256], P(('dp', 'tensor'))
- grad_w_value: float32 [1536, 256], P(('dp', 'tensor'))
- grad_b_value: float32 [256], P(('dp', 'tensor'))
- grad_w_out: float32 [1536, 1536], P('dp', 'tensor')
- grad_mlp_gain: float32 [1536], P(('dp', 'tensor'))
- grad_w_gate: float32 [1536, 8960], P('dp', 'tensor')
- grad_w_up: float32 [1536, 8960], P('dp', 'tensor')
- grad_w_down: float32 [1536, 8960], P('dp', 'tensor')
All inputs are finite; a program needn't handle non-finite values.
Results may differ from a plain program's by a relative error of at most 0.04.
Values may be sent and summed in bfloat16 or wider, within the bound.
A program may use at most 192 MiB of HBM per device.

v0:
```python
from functools import reduce
import math

import jax
import jax.numpy as jnp
from jax import lax
from jax.sharding import PartitionSpec as P

HD = 128
CLEN = 512
GROUPS = 4


EPS = 1e-06
BASE = 1000000.0
NEG = -1e30


def from_behind(x, axis, by):
    size = lax.axis_size(axis)
    pairs = [(i, i + by) for i in range(size) if 0 <= i + by < size]
    return lax.ppermute(x, axis, pairs)


def swapped(value, axis, apart):
    mask = 2**apart
    pairs = [(source, source ^ mask) for source in range(lax.axis_size(axis))]
    return lax.ppermute(value, axis, pairs)


def normed(rows, gain):
    return rows * lax.rsqrt(jnp.mean(rows * rows, -1, keepdims=True) + EPS) * gain


def tables(position, head_dim):
    freq = BASE ** (-(jnp.arange(head_dim // 2, dtype=jnp.float32) * 2.0 / head_dim))
    angle = position.astype(jnp.float32)[:, None] * freq[None, :]
    return (
        jnp.concatenate([jnp.cos(angle), jnp.cos(angle)], -1),
        jnp.concatenate([jnp.sin(angle), jnp.sin(angle)], -1),
    )


def rotate(values, cosine, sine):
    half = values.shape[-1] // 2
    turned = jnp.concatenate([-values[..., half:], values[..., :half]], -1)
    return values * cosine + turned * sine


def layout(start, count, group_tok, prompt):
    index = start + jnp.arange(count, dtype=jnp.int32)
    local = index % group_tok
    later = jnp.maximum(local - prompt, 0)
    in_prompt = local < prompt
    position = jnp.where(in_prompt, local, prompt + later % CLEN)
    segment = jnp.where(in_prompt, 0, 1 + later // CLEN)
    return (position, segment)


def activation(gate_in, up_in):
    return jax.nn.silu(gate_in) * up_in


def block_scores(queries, keys_block, allowed):
    scores = jnp.einsum("hqd,kd->hqk", queries, keys_block, preferred_element_type=jnp.float32) * (
        1.0 / math.sqrt(HD)
    )
    if allowed is None:
        return scores
    return jnp.where(allowed[None], scores, NEG)


def block_peak(queries, keys_block, allowed):
    scores = block_scores(queries, keys_block, allowed)
    peak = jnp.max(scores, -1)
    return (peak, jnp.sum(jnp.exp(scores - peak[..., None]), -1))


def block_mix(queries, keys_block, values_block, allowed, spread):
    probs = jnp.exp(block_scores(queries, keys_block, allowed) - spread[..., None]).astype(
        jnp.bfloat16
    )
    return jnp.einsum("hqk,kd->hqd", probs, values_block, preferred_element_type=jnp.float32)


def block_back(queries, keys_block, values_block, allowed, spread, d_mixed, offset_terms):
    probs = jnp.exp(block_scores(queries, keys_block, allowed) - spread[..., None])
    d_values = jnp.einsum(
        "hqk,hqd->kd", probs.astype(jnp.bfloat16), d_mixed, preferred_element_type=jnp.float32
    )
    d_probs = jnp.einsum("hqd,kd->hqk", d_mixed, values_block, preferred_element_type=jnp.float32)
    d_scores = (probs * (d_probs - offset_terms[..., None])).astype(jnp.bfloat16)
    scale = 1.0 / math.sqrt(HD)
    d_queries = (
        jnp.einsum("hqk,kd->hqd", d_scores, keys_block, preferred_element_type=jnp.float32) * scale
    )
    d_keys = (
        jnp.einsum("hqk,hqd->kd", d_scores, queries, preferred_element_type=jnp.float32) * scale
    )
    return (d_queries, jnp.concatenate([d_keys, d_values], 1))


def reduce_weights(terms):
    return (
        lax.psum_scatter(
            terms[0].astype(jnp.bfloat16), "dp", scatter_dimension=0, tiled=True
        ).astype(jnp.float32),
        lax.psum_scatter(
            terms[1].astype(jnp.bfloat16), "dp", scatter_dimension=0, tiled=True
        ).astype(jnp.float32),
        lax.psum_scatter(
            terms[2].astype(jnp.bfloat16), "dp", scatter_dimension=0, tiled=True
        ).astype(jnp.float32),
        lax.psum_scatter(
            terms[3].astype(jnp.bfloat16), "dp", scatter_dimension=0, tiled=True
        ).astype(jnp.float32),
        lax.psum_scatter(
            terms[4].astype(jnp.bfloat16), "dp", scatter_dimension=0, tiled=True
        ).astype(jnp.float32),
    )


def shards(
    tokens,
    grad_out,
    attn_gain,
    w_query,
    b_query,
    w_key,
    b_key,
    w_value,
    b_value,
    w_out,
    mlp_gain,
    w_gate,
    w_up,
    w_down,
):
    tensor_count = lax.axis_size("tensor")
    data_count = lax.axis_size("dp")
    tensor_index = lax.axis_index("tensor")
    data_index = lax.axis_index("dp")
    rows = tokens.shape[0] * tensor_count
    members = data_count // GROUPS
    group_tok = members * rows
    prompt = group_tok // 2
    offset = data_index % members
    query_width = w_query.shape[1]
    heads = query_width // HD
    key_width = w_key.shape[1]
    key_head = tensor_index // (tensor_count // (key_width // HD))
    width_model = tokens.shape[1]
    inputs = tokens.astype(jnp.float32)
    normal_in = normed(inputs, attn_gain)
    rows_in, rows_grad = (
        lax.all_gather(normal_in.astype(jnp.bfloat16), "tensor", axis=0, tiled=True),
        lax.all_gather(grad_out, "tensor", axis=0, tiled=True),
    )
    key_cols = lax.dynamic_slice_in_dim(w_key, key_head * HD, HD, 1)
    value_cols = lax.dynamic_slice_in_dim(w_value, key_head * HD, HD, 1)
    pair_cols = jnp.concatenate([key_cols, value_cols], 1)
    full_query, full_pair, full_out, full_gate, full_up, full_down = (
        lax.all_gather(w_query, "dp", axis=0, tiled=True),
        lax.all_gather(pair_cols, "dp", axis=0, tiled=True),
        lax.all_gather(w_out, "dp", axis=0, tiled=True),
        lax.all_gather(w_gate, "dp", axis=0, tiled=True),
        lax.all_gather(w_up, "dp", axis=0, tiled=True),
        lax.all_gather(w_down, "dp", axis=0, tiled=True),
    )
    query_bias = lax.dynamic_slice_in_dim(b_query, tensor_index * query_width, query_width, 0)
    pair_bias = jnp.concatenate(
        [
            lax.dynamic_slice_in_dim(b_key, key_head * HD, HD, 0),
            lax.dynamic_slice_in_dim(b_value, key_head * HD, HD, 0),
        ]
    )
    query_lin = jnp.dot(rows_in, full_query, preferred_element_type=jnp.float32) + query_bias
    pair_lin = jnp.dot(rows_in, full_pair, preferred_element_type=jnp.float32) + pair_bias
    position, segment = layout(data_index * rows, rows, group_tok, prompt)
    cosine, sine = tables(position, HD)

    def turned(values):
        return rotate(values, cosine, sine)

    query_heads = query_lin.reshape(rows, heads, HD).transpose(1, 0, 2)
    key_lin = pair_lin[:, :HD]
    queries = turned(query_heads).astype(jnp.bfloat16)
    keys = turned(key_lin).astype(jnp.bfloat16)
    values = pair_lin[:, HD:].astype(jnp.bfloat16)
    allowed = (position[None, :] <= position[:, None]) & (
        (segment[None, :] == 0) | (segment[None, :] == segment[:, None])
    )
    remote = []
    for step in range(1, members):
        keys_far, values_far = from_behind((keys, values), "dp", step)
        usable = (offset >= step) & (offset - step < members // 2)
        remote.append((keys_far, values_far, usable))
    empty_peak = jnp.full((heads, rows), NEG, jnp.float32)
    empty_total = jnp.zeros((heads, rows), jnp.float32)
    empty_mix = jnp.zeros((heads, rows, HD), jnp.float32)

    def far_peak(keys_block):
        return block_peak(queries, keys_block, None)

    def skip_peak(keys_block):
        return (empty_peak, empty_total)

    peaks = [block_peak(queries, keys, allowed)]
    for keys_far, values_far, usable in remote:
        peaks.append(lax.cond(usable, far_peak, skip_peak, keys_far))
    peak = reduce(jnp.maximum, [entry[0] for entry in peaks])
    total = reduce(jnp.add, [entry[1] * jnp.exp(entry[0] - peak) for entry in peaks])
    spread = peak + jnp.log(total)

    def far_mix(keys_block, values_block):
        return block_mix(queries, keys_block, values_block, None, spread)

    def skip_mix(keys_block, values_block):
        return empty_mix

    mixed = block_mix(queries, keys, values, allowed, spread)
    for keys_far, values_far, usable in remote:
        mixed = mixed + lax.cond(usable, far_mix, skip_mix, keys_far, values_far)
    mixed_rows = mixed.transpose(1, 0, 2).reshape(rows, query_width).astype(jnp.bfloat16)
    branch = jnp.einsum("rq,dq->rd", mixed_rows, full_out, preferred_element_type=jnp.float32)
    middle = inputs + lax.psum_scatter(
        branch.astype(jnp.bfloat16), "tensor", scatter_dimension=0, tiled=True
    ).astype(jnp.float32)
    normal_mid = normed(middle, mlp_gain)
    rows_mid = lax.all_gather(normal_mid.astype(jnp.bfloat16), "tensor", axis=0, tiled=True)
    gate = jnp.dot(rows_mid, full_gate, preferred_element_type=jnp.float32)
    up = jnp.dot(rows_mid, full_up, preferred_element_type=jnp.float32)
    hidden = activation(gate, up).astype(jnp.bfloat16)
    down_part = jnp.einsum("rf,df->rd", hidden, full_down, preferred_element_type=jnp.float32)
    result = middle + lax.psum_scatter(
        down_part.astype(jnp.bfloat16), "tensor", scatter_dimension=0, tiled=True
    ).astype(jnp.float32)
    back_query, back_pair, back_out, back_gate, back_up, back_down = (
        lax.all_gather(w_query, "dp", axis=0, tiled=True),
        lax.all_gather(pair_cols, "dp", axis=0, tiled=True),
        lax.all_gather(w_out, "dp", axis=0, tiled=True),
        lax.all_gather(w_gate, "dp", axis=0, tiled=True),
        lax.all_gather(w_up, "dp", axis=0, tiled=True),
        lax.all_gather(w_down, "dp", axis=0, tiled=True),
    )
    d_hidden = jnp.dot(rows_grad, back_down, preferred_element_type=jnp.float32)
    grad_down = jnp.einsum("rd,rf->df", rows_grad, hidden, preferred_element_type=jnp.float32)
    d_gate, d_up = jax.vjp(activation, gate, up)[1](d_hidden)
    d_gate = d_gate.astype(jnp.bfloat16)
    d_up = d_up.astype(jnp.bfloat16)
    grad_gate = jnp.einsum("rd,rf->df", rows_mid, d_gate, preferred_element_type=jnp.float32)
    grad_up = jnp.einsum("rd,rf->df", rows_mid, d_up, preferred_element_type=jnp.float32)
    d_mid_rows = jnp.einsum(
        "rf,df->rd", d_gate, back_gate, preferred_element_type=jnp.float32
    ) + jnp.einsum("rf,df->rd", d_up, back_up, preferred_element_type=jnp.float32)
    d_mid = lax.psum_scatter(
        d_mid_rows.astype(jnp.bfloat16), "tensor", scatter_dimension=0, tiled=True
    ).astype(jnp.float32)
    d_middle_norm, grad_mlp_gain = jax.vjp(normed, middle, mlp_gain)[1](d_mid)
    d_middle = grad_out.astype(jnp.float32) + d_middle_norm
    rows_back = lax.all_gather(d_middle.astype(jnp.bfloat16), "tensor", axis=0, tiled=True)
    grad_proj = jnp.einsum("rd,rq->dq", rows_back, mixed_rows, preferred_element_type=jnp.float32)
    d_mixed_rows = jnp.dot(rows_back, back_out, preferred_element_type=jnp.float32).astype(
        jnp.bfloat16
    )
    d_mixed = d_mixed_rows.reshape(rows, heads, HD).transpose(1, 0, 2)
    offset_terms = jnp.sum(d_mixed.astype(jnp.float32) * mixed, -1)

    def far_back(keys_block, values_block):
        return block_back(queries, keys_block, values_block, None, spread, d_mixed, offset_terms)

    def skip_back(keys_block, values_block):
        return (empty_mix, jnp.zeros((rows, 2 * HD), jnp.float32))

    d_queries, d_pair = block_back(queries, keys, values, allowed, spread, d_mixed, offset_terms)
    for step, entry in enumerate(remote, 1):
        part_queries, part_pair = lax.cond(entry[2], far_back, skip_back, entry[0], entry[1])
        d_queries = d_queries + part_queries
        d_pair = d_pair + from_behind(part_pair.astype(jnp.bfloat16), "dp", -step).astype(
            part_pair.dtype
        )
    d_pair = d_pair + swapped(d_pair.astype(jnp.bfloat16), "tensor", 0).astype(d_pair.dtype)
    d_key = jax.vjp(turned, key_lin)[1](d_pair[:, :HD])[0]
    pair_low = jnp.concatenate([d_key, d_pair[:, HD:]], 1).astype(jnp.bfloat16)
    d_query_heads = jax.vjp(turned, query_heads)[1](d_queries)[0]
    d_query = d_query_heads.transpose(1, 0, 2).reshape(rows, query_width).astype(jnp.bfloat16)
    which = tensor_index % 2
    mine = lax.dynamic_slice_in_dim(pair_low, which * HD, HD, 1)
    mine_weight = lax.dynamic_slice_in_dim(back_pair, which * HD, HD, 1)
    grad_query = jnp.einsum("rd,rq->dq", rows_in, d_query, preferred_element_type=jnp.float32)
    grad_mine = jnp.einsum("rd,rk->dk", rows_in, mine, preferred_element_type=jnp.float32)
    d_in_rows = jnp.einsum(
        "rq,dq->rd", d_query, back_query, preferred_element_type=jnp.float32
    ) + jnp.einsum("rk,dk->rd", mine, mine_weight, preferred_element_type=jnp.float32)
    d_in = lax.psum_scatter(
        d_in_rows.astype(jnp.bfloat16), "tensor", scatter_dimension=0, tiled=True
    ).astype(jnp.float32)
    d_in_norm, grad_attn_gain = jax.vjp(normed, inputs, attn_gain)[1](d_in)
    grad_in = d_middle + d_in_norm
    column = which * key_width + key_head * HD
    pair_grad = lax.dynamic_update_slice(
        jnp.zeros((width_model, 2 * key_width), jnp.float32), grad_mine, (0, column)
    )
    bias_grad = lax.dynamic_update_slice(
        jnp.zeros((2 * key_width,), jnp.float32), jnp.sum(mine.astype(jnp.float32), 0), (column,)
    )
    query_bias_grad = lax.dynamic_update_slice(
        jnp.zeros((b_query.shape[0],), jnp.float32),
        jnp.sum(d_query.astype(jnp.float32), 0),
        (tensor_index * query_width,),
    )
    shared = (
        lax.psum_scatter(
            pair_grad[:, :key_width], ("dp", "tensor"), scatter_dimension=0, tiled=True
        ),
        lax.psum_scatter(
            pair_grad[:, key_width:], ("dp", "tensor"), scatter_dimension=0, tiled=True
        ),
        lax.psum_scatter(query_bias_grad, ("dp", "tensor"), scatter_dimension=0, tiled=True),
        lax.psum_scatter(bias_grad[:key_width], ("dp", "tensor"), scatter_dimension=0, tiled=True),
        lax.psum_scatter(bias_grad[key_width:], ("dp", "tensor"), scatter_dimension=0, tiled=True),
        lax.psum_scatter(grad_attn_gain, ("dp", "tensor"), scatter_dimension=0, tiled=True),
        lax.psum_scatter(grad_mlp_gain, ("dp", "tensor"), scatter_dimension=0, tiled=True),
    )
    part_query, part_proj, part_gate, part_up, part_down = reduce_weights(
        (grad_query, grad_proj, grad_gate, grad_up, grad_down)
    )
    return (
        result,
        grad_in,
        shared[5],
        part_query,
        shared[2],
        shared[0],
        shared[3],
        shared[1],
        shared[4],
        part_proj,
        shared[6],
        part_gate,
        part_up,
        part_down,
    )


def solution(mesh):
    return jax.shard_map(
        shards,
        mesh=mesh,
        in_specs=(
            P(("dp", "tensor"), None),
            P(("dp", "tensor"), None),
            P(),
            P("dp", "tensor"),
            P(),
            P("dp", None),
            P(),
            P("dp", None),
            P(),
            P("dp", "tensor"),
            P(),
            P("dp", "tensor"),
            P("dp", "tensor"),
            P("dp", "tensor"),
        ),
        out_specs=(
            P(("dp", "tensor"), None),
            P(("dp", "tensor"), None),
            P(("dp", "tensor")),
            P("dp", "tensor"),
            P(("dp", "tensor")),
            P(("dp", "tensor"), None),
            P(("dp", "tensor")),
            P(("dp", "tensor"), None),
            P(("dp", "tensor")),
            P("dp", "tensor"),
            P(("dp", "tensor")),
            P("dp", "tensor"),
            P("dp", "tensor"),
            P("dp", "tensor"),
        ),
        check_vma=False,
    )
```

profile of v0, /device:TPU:10, one launch (start us, length us, event | category | flops | bytes accessed | tf_op | source)
XLA Modules:
  0.0 1065.4 jit_solution(10550663077449387391)
XLA Ops:
  8.4 1.9 fusion.35
  12.9 10.4 all_gather.38
  25.9 21.8 %all-gather.10.cloned.1.call-done = bf16[512,1536]{1,0:T(8,128)(2,1)} async-done(((bf16[128,1536]{1,0:T(8,128)(2,1)}), bf16[512,1536]{1,0:T(8,128)(2,1)}) %all-gather.10.cloned.1.call-update) | async-done | bytes 1572880 | tf_op jit(solution)/shard_map/all_gather | solution.py:156
  47.7 2.1 convolution_add_fusion.3
  51.5 1.9 collective-permute-start
  53.4 3.5 collective-permute-start.1
  56.9 16.8 %all-gather.12.cloned.1.call-done = bf16[1536,384]{1,0:T(8,128)(2,1)} async-done(((bf16[192,384]{1,0:T(8,128)(2,1)}), bf16[1536,384]{1,0:T(8,128)(2,1)}) %all-gather.12.cloned.1.call-update) | async-done | bytes 1179664 | tf_op jit(solution)/shard_map/all_gather | solution.py:163
  73.7 2.1 convolution_add_fusion.2
  76.8 1.7 fusion.29
  78.5 1.3 exponential_reduce_fusion.1
  82.2 3.4 fusion.80
  85.6 14.1 %all-gather.14.cloned.1.call-done = bf16[1536,384]{1,0:T(8,128)(2,1)} async-done(((bf16[192,384]{1,0:T(8,128)(2,1)}), bf16[1536,384]{1,0:T(8,128)(2,1)}) %all-gather.14.cloned.1.call-update) | async-done | bytes 1179664 | tf_op jit(solution)/shard_map/all_gather | solution.py:165
  99.7 3.6 convolution_convert_fusion.4
  103.3 34.3 %reduce-scatter.14.cloned.1.call-done = bf16[128,1536]{1,0:T(8,128)(2,1)} async-done(((bf16[512,1536]{1,0:T(8,128)(2,1)}), bf16[128,1536]{1,0:T(8,128)(2,1)}) %reduce-scatter.14.cloned.1.call-update) | async-done | bytes 393232 | tf_op jit(solution)/shard_map/reduce_scatter | solution.py:226
  139.9 1.9 multiply_convert_fusion.4
  145.1 33.0 %all-gather.16.cloned.1.call-done = bf16[512,1536]{1,0:T(8,128)(2,1)} async-done(((bf16[128,1536]{1,0:T(8,128)(2,1)}), bf16[512,1536]{1,0:T(8,128)(2,1)}) %all-gather.16.cloned.1.call-update) | async-done | bytes 1572880 | tf_op jit(solution)/shard_map/all_gather | solution.py:230
  178.1 50.5 %all-gather.18.cloned.1.call-done = bf16[1536,2240]{1,0:T(8,128)(2,1)} async-done(((bf16[192,2240]{1,0:T(8,128)(2,1)}), bf16[1536,2240]{1,0:T(8,128)(2,1)}) %all-gather.18.cloned.1.call-update) | async-done | bytes 6881296 | tf_op jit(solution)/shard_map/all_gather | solution.py:166
  228.6 9.4 fusion.83
  238.0 41.4 %all-gather.20.cloned.1.call-done = bf16[1536,2240]{1,0:T(8,128)(2,1)} async-done(((bf16[192,2240]{1,0:T(8,128)(2,1)}), bf16[1536,2240]{1,0:T(8,128)(2,1)}) %all-gather.20.cloned.1.call-update) | async-done | bytes 6881296 | tf_op jit(solution)/shard_map/all_gather | solution.py:167
  279.4 9.5 fusion.84
  288.8 28.2 %all-gather.24.cloned.1.call-done = bf16[512,1536]{1,0:T(8,128)(2,1)} async-done(((bf16[128,1536]{1,0:T(8,128)(2,1)}), bf16[512,1536]{1,0:T(8,128)(2,1)}) %all-gather.24.cloned.1.call-update) | async-done | bytes 1572880 | tf_op jit(solution)/shard_map/all_gather | solution.py:157
  317.0 50.7 %all-gather.22.cloned.1.call-done = bf16[1536,2240]{1,0:T(8,128)(2,1)} async-done(((bf16[192,2240]{1,0:T(8,128)(2,1)}), bf16[1536,2240]{1,0:T(8,128)(2,1)}) %all-gather.22.cloned.1.call-update) | async-done | bytes 6881296 | tf_op jit(solution)/shard_map/all_gather | solution.py:168
  367.7 13.4 %multiply_convert_fusion.1 = (bf16[512,2240]{0,1:T(8,128)(2,1)S(1)}, bf16[512,2240]{0,1:T(8,128)(2,1)S(1)}, bf16[512,2240]{0,1:T(8,128)(2,1)}) fusion(f32[512,2240]{0,1:T(8,128)} %fusion.83, f32[512,2240]{0,1:T(8,128)} %fusion.84, bf16[512,1536]{1,0:T(8,128)(2,1)} %all-gather.24.cloned.1.call-done, bf16[1536,2240]{1,0:T(8,128)(2,1)} %all-gather.22.cloned.1.call-done), kind=kOutput, calls=%fused_computation.33 | convolution fusion | flops 3541565440 | bytes 24510464 | tf_op jit(solution)/shard_map/dot_general | solution.py:246
  381.2 7.8 fusion.85
  389.0 5.0 fusion.27
  394.1 34.3 %reduce-scatter.18.cloned.1.call-done = bf16[128,1536]{1,0:T(8,128)(2,1)} async-done(((bf16[512,1536]{1,0:T(8,128)(2,1)}), bf16[128,1536]{1,0:T(8,128)(2,1)}) %reduce-scatter.18.cloned.1.call-update) | async-done | bytes 393232 | tf_op jit(solution)/shard_map/reduce_scatter | solution.py:256
  428.4 2.1 fusion.37
  431.7 2.3 fusion.74
  434.1 36.2 %all-gather.26.cloned.1.call-done = bf16[512,1536]{1,0:T(8,128)(2,1)} async-done(((bf16[128,1536]{1,0:T(8,128)(2,1)}), bf16[512,1536]{1,0:T(8,128)(2,1)}) %all-gather.26.cloned.1.call-update) | async-done | bytes 1572880 | tf_op jit(solution)/shard_map/all_gather | solution.py:261
  470.3 3.4 convolution_convert_fusion.7
  473.7 1.7 multiply_reduce_fusion.1
  475.4 1.7 conditional.5
  477.2 11.0 %collective-permute-start.2 = (bf16[512,256]{0,1:T(8,128)(2,1)}, bf16[512,256]{0,1:T(8,128)(2,1)}, u32[]{:S(2)}, u32[]{:S(2)}) collective-permute-start(bf16[512,256]{0,1:T(8,128)(2,1)} %get-tuple-element.60), channel_id=1, source_target_pairs={{4,0},{8,4},{12,8},{16,12},{20,16},{24,20},{28,24},{5,1},{9,5},{13... | collective-permute-start | bytes 786440 | tf_op jit(solution)/shard_map/ppermute | solution.py:22
  488.2 3.5 convolution_convert_fusion.5
  492.0 2.2 multiply_convert_fusion.3
  494.3 2.2 broadcast_multiply_fusion
  496.6 2.0 convert_reduce_fusion
  499.4 2.0 convolution_convert_fusion.6
  501.4 2.8 convolution_bitcast_fusion.1
  504.3 2.3 fusion.30
  507.6 1.7 collective-permute-start.3
  510.4 5.4 collective-permute-done.3
  517.2 1.8 fusion.26
  519.1 8.8 convolution_convert_fusion.3
  528.0 7.4 fusion.21
  535.4 10.1 copy.95
  546.9 7.6 convolution_convert_fusion.2
  554.6 7.6 convolution_convert_fusion.1
  564.3 2.0 fusion.76
  567.3 1.6 convert_element_type.202
  569.8 1.6 convert_element_type.198
  571.4 35.3 %reduce-scatter.20.cloned.1.call-done = bf16[128,1536]{1,0:T(8,128)(2,1)} async-done(((bf16[512,1536]{1,0:T(8,128)(2,1)}), bf16[128,1536]{1,0:T(8,128)(2,1)}) %reduce-scatter.20.cloned.1.call-update) | async-done | bytes 393232 | tf_op jit(solution)/shard_map/reduce_scatter | solution.py:295
  606.8 1.4 fusion.38
  608.1 43.9 %all-reduce.9 = (f32[1536]{0:T(1024)S(1)}, f32[1536]{0:T(1024)S(1)}, f32[256]{0:T(256)S(1)}, f32[256]{0:T(256)S(1)}, f32[1536]{0:T(1024)S(1)}) all-reduce(f32[1536]{0:T(1024)S(1)} %get-tuple-element.117, f32[1536]{0:T(1024)S(1)} %bitcast_dynamic-update-slice_fusion, ...), channel_id=6, replica_groups=mesh['dp'=8,'tensor'=4] {'dp','tensor'}, use_global_device_ids=true, to_apply=%region_20.21.clone | all-reduce | flops 5120 | bytes 40960
  655.1 2.9 fusion.40
  657.9 55.8 %reduce-scatter.34.cloned.1.call-done = bf16[192,2240]{1,0:T(8,128)(2,1)} async-done(((bf16[1536,2240]{1,0:T(8,128)(2,1)}), bf16[192,2240]{1,0:T(8,128)(2,1)}) %reduce-scatter.34.cloned.1.call-update) | async-done | bytes 860176
  713.8 1.7 copy.96
  715.5 1.7 copy.69
  717.1 65.9 %reduce-scatter.30.cloned.1.call-done = bf16[192,2240]{1,0:T(8,128)(2,1)} async-done(((bf16[1536,2240]{1,0:T(8,128)(2,1)}), bf16[192,2240]{1,0:T(8,128)(2,1)}) %reduce-scatter.30.cloned.1.call-update) | async-done | bytes 860176 | tf_op jit(solution)/shard_map/reduce_scatter | solution.py:111
  783.1 2.5 convert_element_type.204
  785.5 66.4 %reduce-scatter.32.cloned.1.call-done = bf16[192,2240]{1,0:T(8,128)(2,1)} async-done(((bf16[1536,2240]{1,0:T(8,128)(2,1)}), bf16[192,2240]{1,0:T(8,128)(2,1)}) %reduce-scatter.32.cloned.1.call-update) | async-done | bytes 860176 | tf_op jit(solution)/shard_map/reduce_scatter | solution.py:114
  851.9 2.5 convert_element_type.206
  854.4 101.2 %reduce-scatter.24.cloned.1.call-done = f32[48,256]{1,0:T(8,128)} async-done(((f32[1536,256]{1,0:T(8,128)}), f32[48,256]{1,0:T(8,128)}) %reduce-scatter.24.cloned.1.call-update) | async-done | bytes 49168 | tf_op jit(solution)/shard_map/reduce_scatter | solution.py:313
  955.6 102.6 %reduce-scatter.26.cloned.1.call-done = f32[48,256]{1,0:T(8,128)} async-done(((f32[1536,256]{1,0:T(8,128)}), f32[48,256]{1,0:T(8,128)}) %reduce-scatter.26.cloned.1.call-update) | async-done | bytes 49168 | tf_op jit(solution)/shard_map/reduce_scatter | solution.py:316
  (192 shorter events, 34.2 us)
Async XLA Ops:
  7.2 16.1 %copy-start.43 = (f32[256]{0:T(256)S(1)}, f32[256]{0:T(256)}, u32[]{:S(2)}) copy-start(f32[256]{0:T(256)} %param.26) | copy-start | bytes 3076
  7.2 16.2 %copy-start.44 = (f32[256]{0:T(256)S(1)}, f32[256]{0:T(256)}, u32[]{:S(2)}) copy-start(f32[256]{0:T(256)} %param.28) | copy-start | bytes 3076
  7.2 40.5 %all-gather.10.cloned.1.call-start = ((), (), s32[]{:S(2)}) async-start(), calls=%async_computation.11 | async-start | bytes 1966080 | tf_op jit(solution)/shard_map/all_gather | solution.py:156
  8.4 4.5 copy-start.37
  8.4 4.5 copy-start.33
  10.4 63.3 %all-gather.12.cloned.1.call-start = ((), (), s32[]{:S(2)}) async-start(), calls=%async_computation.12 | async-start | bytes 1327104 | tf_op jit(solution)/shard_map/all_gather | solution.py:163
  11.1 88.6 %all-gather.14.cloned.1.call-start = ((), (), s32[]{:S(2)}) async-start(), calls=%async_computation.13 | async-start | bytes 1327104 | tf_op jit(solution)/shard_map/all_gather | solution.py:165
  11.8 125.8 %reduce-scatter.14.cloned.1.call-start = ((), (), s32[]{:S(2)}) async-start(), calls=%async_computation.14 | async-start | bytes 1966080 | tf_op jit(solution)/shard_map/reduce_scatter | solution.py:226
  23.3 27.4 %copy-start.13 = (bf16[1536,256]{1,0:T(8,128)(2,1)}, bf16[1536,256]{1,0:T(8,128)(2,1)S(1)}, u32[]{:S(2)}) copy-start(bf16[1536,256]{1,0:T(8,128)(2,1)S(1)} %all_gather.38) | copy-start | bytes 2359300
  24.0 51.8 %copy-start.22 = (f32[512,64]{0,1:T(8,128)}, f32[512,64]{0,1:T(8,128)S(1)}, u32[]{:S(2)}) copy-start(f32[512,64]{0,1:T(8,128)S(1)} %get-tuple-element.149) | copy-start | bytes 393220
  24.0 51.8 %copy-start.24 = (f32[512,64]{0,1:T(8,128)}, f32[512,64]{0,1:T(8,128)S(1)}, u32[]{:S(2)}) copy-start(f32[512,64]{0,1:T(8,128)S(1)} %get-tuple-element.148) | copy-start | bytes 393220
  47.7 26.0 %copy-start.18 = (bf16[512,1536]{1,0:T(8,128)(2,1)S(1)}, bf16[512,1536]{1,0:T(8,128)(2,1)}, u32[]{:S(2)}) copy-start(bf16[512,1536]{1,0:T(8,128)(2,1)} %all-gather.10.cloned.1.call-done) | copy-start | bytes 4718596
  51.5 24.5 %copy-start.9 = (f32[512,128]{0,1:T(8,128)}, f32[512,128]{0,1:T(8,128)S(1)}, u32[]{:S(2)}) copy-start(f32[512,128]{0,1:T(8,128)S(1)} %get-tuple-element.146) | copy-start | bytes 786436
  51.5 24.5 %copy-start.11 = (f32[512,128]{0,1:T(8,128)}, f32[512,128]{0,1:T(8,128)S(1)}, u32[]{:S(2)}) copy-start(f32[512,128]{0,1:T(8,128)S(1)} %get-tuple-element.147) | copy-start | bytes 786436
  51.5 28.4 %collective-permute-start = (bf16[512,128]{0,1:T(8,128)(2,1)}, bf16[512,128]{0,1:T(8,128)(2,1)}, u32[]{:S(2)}, u32[]{:S(2)}) collective-permute-start(bf16[512,128]{0,1:T(8,128)(2,1)} %get-tuple-element.145), channel_id=1, source_target_pairs={{0,4},{4,8},{8,12},{12,16},{16,20},{20,24},{24,28},{1,5},{5,9},{9,... | collective-permute-start | bytes 393224 | tf_op jit(solution)/shard_map/ppermute | solution.py:22
  53.4 27.8 %collective-permute-start.1 = (bf16[512,128]{0,1:T(8,128)(2,1)}, bf16[512,128]{0,1:T(8,128)(2,1)}, u32[]{:S(2)}, u32[]{:S(2)}) collective-permute-start(bf16[512,128]{0,1:T(8,128)(2,1)} %slice.74), channel_id=1, source_target_pairs={{0,4},{4,8},{8,12},{12,16},{16,20},{20,24},{24,28},{1,5},{5,9},{9,... | collective-permute-start | bytes 393224 | tf_op jit(solution)/shard_map/ppermute | solution.py:22
  76.8 4.4 copy-start.1
  85.6 52.1 %copy-start = (bf16[128,1536]{1,0:T(8,128)(2,1)S(1)}, bf16[128,1536]{1,0:T(8,128)(2,1)}, u32[]{:S(2)}) copy-start(bf16[128,1536]{1,0:T(8,128)(2,1)} %param.20) | copy-start | bytes 1179652
  85.6 54.3 %copy-start.27 = (f32[1536]{0:T(1024)S(1)}, f32[1536]{0:T(1024)}, u32[]{:S(2)}) copy-start(f32[1536]{0:T(1024)} %param.30) | copy-start | bytes 18436
  103.3 74.8 %all-gather.16.cloned.1.call-start = ((), (), s32[]{:S(2)}) async-start(), calls=%async_computation.15 | async-start | bytes 1966080 | tf_op jit(solution)/shard_map/all_gather | solution.py:230
  141.8 86.8 %all-gather.18.cloned.1.call-start = ((), (), s32[]{:S(2)}) async-start(), calls=%async_computation.16 | async-start | bytes 7962624 | tf_op jit(solution)/shard_map/all_gather | solution.py:166
  142.4 137.0 %all-gather.20.cloned.1.call-start = ((), (), s32[]{:S(2)}) async-start(), calls=%async_computation.17 | async-start | bytes 7962624 | tf_op jit(solution)/shard_map/all_gather | solution.py:167
  143.1 173.9 %all-gather.24.cloned.1.call-start = ((), (), s32[]{:S(2)}) async-start(), calls=%async_computation.20 | async-start | bytes 1966080 | tf_op jit(solution)/shard_map/all_gather | solution.py:157
  143.9 223.8 %all-gather.22.cloned.1.call-start = ((), (), s32[]{:S(2)}) async-start(), calls=%async_computation.18 | async-start | bytes 7962624 | tf_op jit(solution)/shard_map/all_gather | solution.py:168
  144.6 283.8 %reduce-scatter.18.cloned.1.call-start = ((), (), s32[]{:S(2)}) async-start(), calls=%async_computation.21 | async-start | bytes 1966080 | tf_op jit(solution)/shard_map/reduce_scatter | solution.py:256
  381.1 7.8 copy-start.46
  381.1 7.9 copy-start.45
  381.2 7.9 copy-start.40
  394.1 76.2 %all-gather.26.cloned.1.call-start = ((), (), s32[]{:S(2)}) async-start(), calls=%async_computation.22 | async-start | bytes 1966080 | tf_op jit(solution)/shard_map/all_gather | solution.py:261
  434.0 133.3 %reduce-scatter.28.cloned.1.call-start = ((), (), s32[]{:S(2)}) async-start(), calls=%async_computation.27 | async-start | bytes 1327104 | tf_op jit(solution)/shard_map/reduce_scatter | solution.py:108
  470.3 3.4 copy-start.8
  470.3 5.2 copy-start.2
  477.2 29.4 %collective-permute-start.2 = (bf16[512,256]{0,1:T(8,128)(2,1)}, bf16[512,256]{0,1:T(8,128)(2,1)}, u32[]{:S(2)}, u32[]{:S(2)}) collective-permute-start(bf16[512,256]{0,1:T(8,128)(2,1)} %get-tuple-element.60), channel_id=1, source_target_pairs={{4,0},{8,4},{12,8},{16,12},{20,16},{24,20},{28,24},{5,1},{9,5},{13... | collective-permute-start | bytes 786440 | tf_op jit(solution)/shard_map/ppermute | solution.py:22
  491.7 78.0 %reduce-scatter.22.cloned.1.call-start = ((), (), s32[]{:S(2)}) async-start(), calls=%async_computation.24 | async-start | bytes 1327104 | tf_op jit(solution)/shard_map/reduce_scatter | solution.py:105
  492.0 2.3 copy-start.12
  494.3 4.4 copy-start.4
  494.3 2.3 copy-start.10
  496.5 2.9 copy-start.19
  504.2 2.4 copy-start.26
  504.2 5.1 copy-start.17
  504.2 5.1 copy-start.21
  504.2 102.6 %reduce-scatter.20.cloned.1.call-start = ((), (), s32[]{:S(2)}) async-start(), calls=%async_computation.23 | async-start | bytes 1966080 | tf_op jit(solution)/shard_map/reduce_scatter | solution.py:295
  507.6 9.3 copy-start.23
  507.6 9.3 copy-start.25
  507.6 8.1 collective-permute-start.3
  510.4 6.9 copy-start.14
  519.0 136.0 %reduce-scatter.16.cloned.1.call-start = ((), (), s32[]{:S(2)}) async-start(), calls=%async_computation.19 | async-start | bytes 1966080 | tf_op jit(solution)/shard_map/reduce_scatter | solution.py:235
  519.0 8.9 copy-start.42
  527.9 185.8 %reduce-scatter.34.cloned.1.call-start = ((), (), s32[]{:S(2)}) async-start(), calls=%async_computation.30 | async-start | bytes 7962624
  545.5 1.4 copy-start.41
  545.5 237.5 %reduce-scatter.30.cloned.1.call-start = ((), (), s32[]{:S(2)}) async-start(), calls=%async_computation.28 | async-start | bytes 7962624 | tf_op jit(solution)/shard_map/reduce_scatter | solution.py:111
  554.6 297.4 %reduce-scatter.32.cloned.1.call-start = ((), (), s32[]{:S(2)}) async-start(), calls=%async_computation.29 | async-start | bytes 7962624 | tf_op jit(solution)/shard_map/reduce_scatter | solution.py:114
  562.2 1.4 copy-start.20
  562.3 393.3 %reduce-scatter.24.cloned.1.call-start = ((), (), s32[]{:S(2)}) async-start(), calls=%async_computation.25 | async-start | bytes 1622016 | tf_op jit(solution)/shard_map/reduce_scatter | solution.py:313
  566.2 40.6 %copy-start.28 = (f32[1536]{0:T(1024)S(1)}, f32[1536]{0:T(1024)}, u32[]{:S(2)}) copy-start(f32[1536]{0:T(1024)} %param.22) | copy-start | bytes 18436
  566.2 40.6 %copy-start.34 = (f32[128]{0:T(128)S(1)}, f32[128]{0:T(128)}, u32[]{:S(2)}) copy-start(f32[128]{0:T(128)} %copy-done.33) | copy-start | bytes 1540
  566.2 41.9 %copy-start.29 = (f32[1536]{0:T(1024)S(1)}, f32[1536]{0:T(1024)}, u32[]{:S(2)}) copy-start(f32[1536]{0:T(1024)} %get-tuple-element.115) | copy-start | bytes 18436
  566.2 88.7 %copy-start.38 = (f32[128]{0:T(128)S(1)}, f32[128]{0:T(128)}, u32[]{:S(2)}) copy-start(f32[128]{0:T(128)} %copy-done.37) | copy-start | bytes 1540
  566.3 88.8 %copy-start.3 = (bf16[128,1536]{1,0:T(8,128)(2,1)S(1)}, bf16[128,1536]{1,0:T(8,128)(2,1)}, u32[]{:S(2)}) copy-start(bf16[128,1536]{1,0:T(8,128)(2,1)} %reduce-scatter.14.cloned.1.call-done) | copy-start | bytes 1179652
  566.3 88.8 %copy-start.6 = (bf16[128,1536]{1,0:T(8,128)(2,1)S(1)}, bf16[128,1536]{1,0:T(8,128)(2,1)}, u32[]{:S(2)}) copy-start(bf16[128,1536]{1,0:T(8,128)(2,1)} %param.21) | copy-start | bytes 1179652
  566.3 88.8 %copy-start.7 = (bf16[128,1536]{1,0:T(8,128)(2,1)S(1)}, bf16[128,1536]{1,0:T(8,128)(2,1)}, u32[]{:S(2)}) copy-start(bf16[128,1536]{1,0:T(8,128)(2,1)} %reduce-scatter.18.cloned.1.call-done) | copy-start | bytes 1179652
  566.3 88.8 %copy-start.31 = (f32[128]{0:T(128)S(1)}, f32[128]{0:T(128)}, u32[]{:S(2)}) copy-start(f32[128]{0:T(128)} %copy-done.30) | copy-start | bytes 1540
  566.3 88.8 %copy-start.36 = (f32[128]{0:T(128)S(1)}, f32[128]{0:T(128)}, u32[]{:S(2)}) copy-start(f32[128]{0:T(128)} %copy-done.35) | copy-start | bytes 1540
  566.3 491.8 %reduce-scatter.26.cloned.1.call-start = ((), (), s32[]{:S(2)}) async-start(), calls=%async_computation.26 | async-start | bytes 1622016 | tf_op jit(solution)/shard_map/reduce_scatter | solution.py:316
  (7 other events, 4.8 us)
Sparse Core Ops, SparseCore 0:
  10.5 37.2 all-gather.9
  49.6 24.0 all-gather.11
  75.6 24.0 all-gather.13
  103.4 34.1 reduce-scatter.13
  141.9 36.1 all-gather.15
  179.8 48.7 all-gather.17
  230.5 48.8 all-gather.19
  280.9 36.0 all-gather.23
  318.9 48.7 all-gather.21
  394.2 34.1 reduce-scatter.17
  434.1 36.1 all-gather.25
  491.9 36.9 reduce-scatter.27
  533.0 36.7 reduce-scatter.21
  572.5 34.2 reduce-scatter.19
  609.5 35.3 reduce-scatter.15
  648.2 65.4 reduce-scatter.33
  717.5 65.4 reduce-scatter.29
  786.4 65.4 reduce-scatter.31
  858.6 96.9 reduce-scatter.23
  962.1 96.0 reduce-scatter.25
where the time goes:
time: 1080 us; the launch traced here: 1070 us
  waiting for transfers between devices  800 us (74%)
  matrix products  111 us (10%)
  blocking collectives  54.3 us (5%)
  other arithmetic  34.7 us (3%)
  local copies, waits for them, and re-layouts  30.1 us (3%)
  starting transfers between devices  19.8 us (2%)
  between operations  15.5 us (1%)
    reduce_scatter x1, waiting for transfers between devices, shards(): lax.psum_scatter(pair_grad[:, key_width:], ('dp', 'tensor'), scatter_dime...  103 us
    reduce_scatter x1, waiting for transfers between devices, shards(): lax.psum_scatter(pair_grad[:, :key_width], ('dp', 'tensor'), scatter_dime...  101 us
    reduce_scatter x1, waiting for transfers between devices, reduce_weights(): lax.psum_scatter(terms[3].astype(jnp.bfloat16), 'dp', scatter_dimension=0...  66.4 us
    reduce_scatter x1, waiting for transfers between devices, reduce_weights(): lax.psum_scatter(terms[2].astype(jnp.bfloat16), 'dp', scatter_dimension=0...  65.9 us
    unnamed x21, waiting for transfers between devices  60.5 us
    all_gather x1, waiting for transfers between devices, shards(): lax.all_gather(w_down, 'dp', axis=0, tiled=True)  50.7 us
    all_gather x1, waiting for transfers between devices, shards(): lax.all_gather(w_gate, 'dp', axis=0, tiled=True)  50.5 us
    unnamed x1, blocking collectives  43.9 us
  transfers between devices with their start and end apart: 24, of which 19 were waited for; matrix products, arithmetic and copies ran while one was open for 12% of the time, Pallas kernels for 0%

commit v1 on v0

--- a/solution.py
+++ b/solution.py
@@ -1,9 +1,12 @@
+import functools
 from functools import reduce
 import math
 
 import jax
 import jax.numpy as jnp
 from jax import lax
+from jax.experimental import pallas as pl
+from jax.experimental.pallas import tpu as pltpu
 from jax.sharding import PartitionSpec as P
 
 HD = 128
@@ -343,9 +346,1160 @@
     )
 
 
+F32 = jnp.float32
+BF16 = jnp.bfloat16
+MESH = pl.DeviceIdType.MESH
+NCH = 2
+HALF = 1152
+
+
+def dot(a, b, ca=1, cb=0):
+    return lax.dot_general(a, b, (((ca,), (cb,)), ((), ())), preferred_element_type=F32)
+
+
+def rcopy(src, dst, send, recv, dev):
+    return pltpu.make_async_remote_copy(
+        src_ref=src, dst_ref=dst, send_sem=send, recv_sem=recv, device_id=dev, device_id_type=MESH
+    )
+
+
+class Place:
+    def __init__(self, depth):
+        self.depth = depth
+        self.dp = lax.axis_index("dp")
+        self.z = lax.axis_index("tensor")
+        self.core = lax.rem(self.dp, 2)
+        self.chip = self.dp // 2
+        x, y = lax.rem(self.chip, 2), self.chip // 2
+        self.xchip = self.chip + 1 - 2 * x
+        self.ychip = self.chip + 2 - 4 * y
+        self.dchip = 3 - self.chip
+        self.sib = (self.chip * 2 + 1 - self.core, self.z)
+        self.xnbr = (self.xchip * 2 + self.core, self.z)
+        self.ynbr = (self.ychip * 2 + self.core, self.z)
+        self.up = (self.dp, self.z + 1)
+        self.down = (self.dp, self.z - 1)
+        self.has_up = self.z < depth - 1
+        self.has_down = self.z > 0
+
+    def greet(self, across):
+        barrier = pltpu.get_barrier_semaphore()
+        others = [self.sib, self.xnbr, self.ynbr]
+        if across:
+            other = 1 - self.core
+            others += [(self.xchip * 2 + other, self.z), (self.ychip * 2 + other, self.z)]
+        for dev in others:
+            pl.semaphore_signal(barrier, inc=1, device_id=dev, device_id_type=MESH)
+
+        @pl.when(self.has_up)
+        def _():
+            pl.semaphore_signal(barrier, inc=1, device_id=self.up, device_id_type=MESH)
+
+        @pl.when(self.has_down)
+        def _():
+            pl.semaphore_signal(barrier, inc=1, device_id=self.down, device_id_type=MESH)
+
+        count = len(others) + self.has_up.astype(jnp.int32) + self.has_down.astype(jnp.int32)
+        pl.semaphore_wait(barrier, count)
+
+
+class LineGather:
+    def __init__(self, place, at, send, recv):
+        self.p, self.at, self.send, self.recv = place, at, send, recv
+
+    def _copy(self, way, ch, d, s):
+        dev = self.p.up if way == 0 else self.p.down
+        block = self.at(ch, s)
+        return rcopy(block, block, self.send.at[way, ch, d], self.recv.at[way, ch, d + 1], dev)
+
+    def own(self, ch):
+        for way, there in ((0, self.p.has_up), (1, self.p.has_down)):
+
+            @pl.when(there)
+            def _(way=way):
+                self._copy(way, ch, 0, self.p.z).start()
+
+    def step(self, ch, d):
+        p = self.p
+        for way in (0, 1):
+            s = p.z - d if way == 0 else p.z + d
+            valid = s >= 0 if way == 0 else s < p.depth
+            onward = p.has_up if way == 0 else p.has_down
+
+            @pl.when(valid)
+            def _(way=way, s=s, onward=onward):
+                block = self.at(ch, s)
+                rcopy(
+                    block, block, self.send.at[way, ch, d - 1], self.recv.at[way, ch, d], p.up
+                ).wait_recv()
+                if d < p.depth - 1:
+
+                    @pl.when(onward)
+                    def _():
+                        self._copy(way, ch, d, s).start()
+
+    def drain(self):
+        p = self.p
+        for ch in range(NCH):
+            for d in range(p.depth - 1):
+                for way in (0, 1):
+                    s = p.z - d if way == 0 else p.z + d
+                    valid = (s >= 0) & p.has_up if way == 0 else (s < p.depth) & p.has_down
+
+                    @pl.when(valid)
+                    def _(way=way, ch=ch, d=d, s=s):
+                        self._copy(way, ch, d, s).wait_send()
+
+
+class LineScatter:
+    def __init__(self, place, part, land, send, recv):
+        self.p, self.part, self.land, self.send, self.recv = place, part, land, send, recv
+
+    def _copy(self, way, ch, d, s):
+        dev = self.p.up if way == 0 else self.p.down
+        return rcopy(
+            self.part(ch, s),
+            self.land.at[way, ch, d - 1],
+            self.send.at[way, ch, d],
+            self.recv.at[way, ch, d - 1],
+            dev,
+        )
+
+    def _arrive(self, way, ch, d):
+        here = self.land.at[way, ch, d]
+        rcopy(here, here, self.send.at[way, ch, d], self.recv.at[way, ch, d], self.p.up).wait_recv()
+
+    def step(self, ch, d):
+        p = self.p
+        for way in (0, 1):
+            s = p.z + d if way == 0 else p.z - d
+            valid = s < p.depth if way == 0 else s >= 0
+            fed = p.has_down if way == 0 else p.has_up
+
+            @pl.when(valid)
+            def _(way=way, s=s, fed=fed):
+                if d < p.depth - 1:
+
+                    @pl.when(fed)
+                    def _():
+                        self._arrive(way, ch, d)
+                        block = self.part(ch, s)
+                        block[...] = (
+                            block[...].astype(F32) + self.land[way, ch, d].astype(F32)
+                        ).astype(BF16)
+
+                self._copy(way, ch, d, s).start()
+
+    def total(self, ch, out):
+        p = self.p
+        out[...] = self.part(ch, p.z)[...].astype(F32)
+        for way, fed in ((0, p.has_down), (1, p.has_up)):
+
+            @pl.when(fed)
+            def _(way=way):
+                self._arrive(way, ch, 0)
+                out[...] += self.land[way, ch, 0].astype(F32)
+
+    def drain(self):
+        p = self.p
+        for ch in range(NCH):
+            for d in range(1, p.depth):
+                for way in (0, 1):
+                    s = p.z + d if way == 0 else p.z - d
+                    valid = s < p.depth if way == 0 else s >= 0
+
+                    @pl.when(valid)
+                    def _(way=way, ch=ch, d=d, s=s):
+                        self._copy(way, ch, d, s).wait_send()
+
+
+def inverse_root(rows):
+    return lax.rsqrt(jnp.mean(rows * rows, -1, keepdims=True) + EPS)
+
+
+def turn(u, cosine, sine_signed):
+    return u * cosine + pltpu.roll(u, HD // 2, 1) * sine_signed
+
+
+def forward_kernel(
+    tokens, grad_out, attn_gain, mlp_gain, w_query, w_key, w_value, w_out, w_gate, w_up, w_down,
+    b_query, b_key, b_value, cosine, sine,
+    big, proj, rows_in, heads_q, pair, mixed, middle, rows_mid, rows_grad,
+    pad, v_proj, v_in, v_pair, v_mixed, v_mid, v_grad, part, land, total,
+    big_send, big_recv, proj_send, proj_recv, own_sem, z_send, z_recv, s_send, s_recv, core_send, core_recv, out_sem,
+):
+    p = Place(4)
+    z, core = p.z, p.core
+    unit = tokens.shape[0] // NCH
+    wide = unit * p.depth
+    shard = w_query.shape[0]
+    q_width = w_query.shape[1]
+
+    def rows_of(ref, ch, s):
+        return ref.at[pl.ds(pl.multiple_of(ch * wide + s * unit, unit), unit), :]
+
+    gather_in = LineGather(p, lambda ch, s: rows_of(v_in, ch, s), z_send.at[0], z_recv.at[0])
+    gather_grad = LineGather(
+        p, lambda ch, s: rows_of(v_grad.at[core], ch, s), z_send.at[1], z_recv.at[1]
+    )
+    gather_mid = LineGather(
+        p, lambda ch, s: rows_of(v_mid.at[core], ch, s), z_send.at[2], z_recv.at[2]
+    )
+    scatter = LineScatter(p, lambda ch, s: rows_of(part, ch, s), land, s_send, s_recv)
+
+    p.greet(True)
+
+    for ch in range(NCH):
+        x = tokens[ch * unit : (ch + 1) * unit, :].astype(F32)
+        a1 = (x * inverse_root(x) * attn_gain[...]).astype(BF16)
+        v_in[pl.ds(pl.multiple_of(ch * wide + z * unit, unit), unit), :] = a1
+        gather_in.own(ch)
+
+    kv = pl.ds(pl.multiple_of((z // 2) * HD, HD), HD)
+    mine = pl.ds(pl.multiple_of(p.dp * shard, 16), shard)
+    v_proj[mine, 0:q_width] = w_query[...]
+    v_proj[mine, q_width : q_width + HD] = w_key[:, kv]
+    v_proj[mine, q_width + HD : q_width + 2 * HD] = w_value[:, kv]
+    v_proj[mine, q_width + 2 * HD :] = w_out[...]
+
+    def proj_rows(dp, first=0, count=shard):
+        return v_proj.at[pl.ds(pl.multiple_of(dp * shard + first, 16), count), :]
+
+    def proj_copy(k, src, dev, first=0, count=shard):
+        block = proj_rows(src, first, count)
+        return rcopy(block, block, proj_send.at[k], proj_recv.at[k], dev)
+
+    half_rows = shard // 2
+    d_dp = p.dchip * 2 + core
+    proj_out = [
+        proj_copy(0, p.dp, p.xnbr),
+        proj_copy(1, p.dp, p.ynbr),
+        proj_copy(2, p.dp, p.sib),
+        proj_copy(3, p.ynbr[0], p.xnbr, 0, half_rows),
+        proj_copy(4, p.xnbr[0], p.ynbr, half_rows, half_rows),
+        proj_copy(5, p.xnbr[0], p.sib),
+        proj_copy(6, p.ynbr[0], p.sib),
+        proj_copy(7, d_dp, p.sib),
+    ]
+    other = 1 - 2 * core
+    proj_in = [
+        proj_copy(0, p.xnbr[0], p.xnbr),
+        proj_copy(1, p.ynbr[0], p.ynbr),
+        proj_copy(2, p.dp + other, p.sib),
+        proj_copy(3, d_dp, p.xnbr, 0, half_rows),
+        proj_copy(4, d_dp, p.ynbr, half_rows, half_rows),
+        proj_copy(5, p.xnbr[0] + other, p.sib),
+        proj_copy(6, p.ynbr[0] + other, p.sib),
+        proj_copy(7, d_dp + other, p.sib),
+    ]
+    for k in range(3):
+        proj_out[k].start()
+
+    tail = w_gate.shape[1] - HALF
+    whole = tail // 128 * 128
+    mats = (w_gate, w_up, w_down)
+    for k, mat in enumerate(mats):
+        pad[k, :, 0:whole] = mat[:, HALF : HALF + whole]
+        pad[k, :, whole:] = jnp.concatenate(
+            [mat[:, HALF + whole :], jnp.zeros((shard, HALF - tail), BF16)], 1
+        )
+
+    def big_rows(k, dp):
+        return big.at[k, pl.ds(pl.multiple_of(dp * shard, 16), shard), :]
+
+    def half_of(k, c):
+        return mats[k].at[:, 0:HALF] if c == 0 else pad.at[k]
+
+    def big_out(k):
+        copies = []
+        for c in (0, 1):
+            for way, chip in ((0, p.xchip), (1, p.ychip)):
+                copies.append(
+                    rcopy(
+                        half_of(k, c),
+                        big_rows(k, p.dp),
+                        big_send.at[k, way, c],
+                        big_recv.at[k, way, core],
+                        (chip * 2 + c, z),
+                    )
+                )
+        return copies
+
+    def big_near(k, c):
+        return rcopy(
+            half_of(k, c), big_rows(k, p.dp), big_send.at[k, 2, 0], big_recv.at[k, 2, 0], p.sib
+        )
+
+    def big_keep(k, c):
+        return pltpu.make_async_copy(half_of(k, c), big_rows(k, p.dp), own_sem.at[k])
+
+    def big_in(k, way, c):
+        dp = (p.xchip if way == 0 else p.ychip) * 2 + c
+        block = big_rows(k, dp)
+        return rcopy(block, block, big_send.at[k, way, c], big_recv.at[k, way, c], p.sib)
+
+    def big_relay(k):
+        one, two = big_rows(k, p.ychip * 2), big_rows(k, p.xchip * 2 + 1)
+        return (
+            rcopy(one, one, big_send.at[k, 3, 0], big_recv.at[k, 3, 0], p.xnbr),
+            rcopy(two, two, big_send.at[k, 3, 1], big_recv.at[k, 3, 1], p.ynbr),
+        )
+
+    def big_start(k):
+        for copy in big_out(k):
+            copy.start()
+        for c in (0, 1):
+
+            @pl.when(core == 1 - c)
+            def _(c=c):
+                big_near(k, c).start()
+
+            @pl.when(core == c)
+            def _(c=c):
+                big_keep(k, c).start()
+
+    def big_forward(k):
+        big_in(k, 1, 0).wait_recv()
+        big_in(k, 0, 1).wait_recv()
+        for copy in big_relay(k):
+            copy.start()
+
+    def big_finish(k):
+        big_in(k, 0, 0).wait_recv()
+        big_in(k, 1, 1).wait_recv()
+        for i, dp in ((0, p.dchip * 2), (1, p.dchip * 2 + 1)):
+            block = big_rows(k, dp)
+            rcopy(block, block, big_send.at[k, 3, i], big_recv.at[k, 3, i], p.sib).wait_recv()
+        block = big_rows(k, p.sib[0])
+        rcopy(block, block, big_send.at[k, 2, 0], big_recv.at[k, 2, 0], p.sib).wait_recv()
+        for copy in big_out(k) + list(big_relay(k)):
+            copy.wait_send()
+        for c in (0, 1):
+
+            @pl.when(core == 1 - c)
+            def _(c=c):
+                big_near(k, c).wait_send()
+
+            @pl.when(core == c)
+            def _(c=c):
+                big_keep(k, c).wait()
+
+    big_start(0)
+    for ch in range(NCH):
+        gather_in.step(ch, 1)
+    for ch in range(NCH):
+        gather_in.step(ch, 2)
+    big_start(1)
+    proj_in[0].wait_recv()
+    proj_out[4].start()
+    proj_out[5].start()
+    proj_in[1].wait_recv()
+    proj_out[3].start()
+    proj_out[6].start()
+    for ch in range(NCH):
+        rows = pl.ds(pl.multiple_of(ch * wide + z * unit, unit), unit)
+        v_grad[core, rows, :] = grad_out[ch * unit : (ch + 1) * unit, :]
+    for ch in range(NCH):
+        gather_in.step(ch, 3)
+    for ch in range(NCH):
+        gather_grad.own(ch)
+    for k in (3, 4):
+        proj_in[k].wait_recv()
+    proj_out[7].start()
+    for k in (2, 5, 6, 7):
+        proj_in[k].wait_recv()
+
+    bias_q = b_query[:, pl.ds(pl.multiple_of(z * q_width, HD), q_width)]
+    bias_k, bias_v = b_key[:, kv], b_value[:, kv]
+    heads = q_width // HD
+    for ch in range(NCH):
+        rows = slice(ch * wide, (ch + 1) * wide)
+        lin = dot(v_in[rows, :], v_proj[:, 0 : q_width + 2 * HD])
+        c, s = cosine[rows, :], sine[rows, :]
+        for h in range(heads):
+            u = lin[:, h * HD : (h + 1) * HD] + bias_q[:, h * HD : (h + 1) * HD]
+            heads_q[h, rows, :] = turn(u, c, s).astype(BF16)
+        v_pair[core, rows, 0:HD] = turn(
+            lin[:, q_width : q_width + HD] + bias_k, c, s
+        ).astype(BF16)
+        v_pair[core, rows, HD:] = (lin[:, q_width + HD :] + bias_v).astype(BF16)
+    pair_out = rcopy(v_pair.at[core], v_pair.at[core], core_send.at[0], core_recv.at[0], p.sib)
+    pair_out.start()
+    pair_in = rcopy(
+        v_pair.at[1 - core], v_pair.at[1 - core], core_send.at[0], core_recv.at[0], p.sib
+    )
+    pair_in.wait_recv()
+
+    for ch in range(NCH):
+
+        def one_head(h, _):
+            keep = allowed(core, ch, unit, p.depth, wide)
+            _, pb = softmax(heads_q[h, ch * wide : (ch + 1) * wide, :], v_pair, keep)
+            o = dot(pb, both(v_pair, HD))
+            v_mixed[ch * wide : (ch + 1) * wide, pl.ds(pl.multiple_of(h * HD, HD), HD)] = o.astype(
+                BF16
+            )
+            return 0
+
+        lax.fori_loop(0, heads, one_head, 0)
+        rows = slice(ch * wide, (ch + 1) * wide)
+        part[rows, :] = dot(v_mixed[rows, :], v_proj[:, q_width + 2 * HD :], 1, 1).astype(BF16)
+        scatter.step(ch, 3)
+    big_forward(0)
+    big_start(2)
+    for ch in range(NCH):
+        gather_grad.step(ch, 1)
+    for ch in range(NCH):
+        scatter.step(ch, 2)
+        scatter.step(ch, 1)
+        scatter.total(ch, total)
+        half = slice(ch * unit, (ch + 1) * unit)
+        mid = tokens[half, :].astype(F32) + total[...]
+        middle[half, :] = mid
+        v_mid[core, pl.ds(pl.multiple_of(ch * wide + z * unit, unit), unit), :] = (
+            mid * inverse_root(mid) * mlp_gain[...]
+        ).astype(BF16)
+        gather_mid.own(ch)
+        if ch == 0:
+            for c in range(NCH):
+                gather_grad.step(c, 2)
+    big_forward(1)
+    for ch in range(NCH):
+        gather_mid.step(ch, 1)
+    for ch in range(NCH):
+        gather_grad.step(ch, 3)
+    for ch in range(NCH):
+        gather_mid.step(ch, 2)
+
+    def near(k, ref, ch, slot):
+        block = ref.at[slot, pl.ds(ch * wide, wide), :]
+        return rcopy(block, block, core_send.at[k], core_recv.at[k], p.sib)
+
+    for ch in range(NCH):
+        near(1 + ch, v_grad, ch, core).start()
+    big_forward(2)
+    for ch in range(NCH):
+        gather_mid.step(ch, 3)
+        near(3 + ch, v_mid, ch, core).start()
+    for ch in range(NCH):
+        near(1 + ch, v_grad, ch, 1 - core).wait_recv()
+        near(3 + ch, v_mid, ch, 1 - core).wait_recv()
+    outs = [
+        pltpu.make_async_copy(src, dst, out_sem.at[i])
+        for i, (src, dst) in enumerate(
+            (
+                (v_proj, proj),
+                (v_in, rows_in),
+                (v_pair, pair),
+                (v_mixed, mixed),
+                (v_mid, rows_mid),
+                (v_grad, rows_grad),
+            )
+        )
+    ]
+    for copy in outs:
+        copy.start()
+    for k in range(3):
+        big_finish(k)
+    for copy in proj_out:
+        copy.wait_send()
+    pair_out.wait_send()
+    for ch in range(NCH):
+        near(1 + ch, v_grad, ch, core).wait_send()
+        near(3 + ch, v_mid, ch, core).wait_send()
+    for line in (gather_in, gather_grad, gather_mid, scatter):
+        line.drain()
+    for copy in outs:
+        copy.wait()
+
+
+def allowed(core, ch, unit, depth, wide):
+    def place_of(row):
+        chunk, rest = row // wide, lax.rem(row, wide)
+        return (rest // unit) * (unit * NCH) + chunk * unit + lax.rem(rest, unit)
+
+    keys = NCH * wide
+    query = lax.broadcasted_iota(jnp.int32, (wide, 2 * keys), 0)
+    key = lax.broadcasted_iota(jnp.int32, (wide, 2 * keys), 1)
+    key_at = (key // keys) * keys + place_of(lax.rem(key, keys))
+    return key_at <= core * keys + place_of(query + ch * wide)
+
+
+def both(pair, first):
+    return pair[:, :, first : first + HD].reshape(-1, HD)
+
+
+def softmax(queries, pair, keep):
+    scores = dot(queries, both(pair, 0), 1, 1) * (1.0 / math.sqrt(HD))
+    scores = jnp.where(keep, scores, NEG)
+    weights = jnp.exp(scores - jnp.max(scores, -1, keepdims=True))
+    probs = weights / jnp.sum(weights, -1, keepdims=True)
+    return probs, probs.astype(BF16)
+
+
+def forward_call(depth, args):
+    rows, width = args[0].shape
+    total_rows = rows * depth
+    shard, q_width = args[4].shape
+    d_model = width
+    unit = rows // NCH
+    vm = pl.BlockSpec(memory_space=pltpu.VMEM)
+    anyspace = pl.BlockSpec(memory_space=pl.ANY)
+    sds = jax.ShapeDtypeStruct
+    dma = pltpu.SemaphoreType.DMA
+    out_shape = (
+        sds((3, d_model, HALF), BF16),
+        sds((d_model, 2 * q_width + 2 * HD), BF16),
+        sds((total_rows, width), BF16),
+        sds((q_width // HD, total_rows, HD), BF16),
+        sds((2, total_rows, 2 * HD), BF16),
+        sds((total_rows, q_width), BF16),
+        sds((rows, width), F32),
+        sds((2, total_rows, width), BF16),
+        sds((2, total_rows, width), BF16),
+    )
+    return pl.pallas_call(
+        forward_kernel,
+        out_shape=out_shape,
+        in_specs=[vm] * len(args),
+        out_specs=(anyspace, anyspace, anyspace, vm, anyspace, anyspace, vm, anyspace, anyspace),
+        scratch_shapes=[
+            pltpu.VMEM((3, shard, HALF), BF16),
+            pltpu.VMEM((d_model, 2 * q_width + 2 * HD), BF16),
+            pltpu.VMEM((total_rows, width), BF16),
+            pltpu.VMEM((2, total_rows, 2 * HD), BF16),
+            pltpu.VMEM((total_rows, q_width), BF16),
+            pltpu.VMEM((2, total_rows, width), BF16),
+            pltpu.VMEM((2, total_rows, width), BF16),
+            pltpu.VMEM((total_rows, width), BF16),
+            pltpu.VMEM((2, NCH, depth - 1, unit, width), BF16),
+            pltpu.VMEM((unit, width), F32),
+            dma((3, 4, 2)),
+            dma((3, 4, 2)),
+            dma((8,)),
+            dma((8,)),
+            dma((3,)),
+            dma((3, 2, NCH, depth)),
+            dma((3, 2, NCH, depth)),
+            dma((2, NCH, depth)),
+            dma((2, NCH, depth)),
+            dma((1 + 2 * NCH,)),
+            dma((1 + 2 * NCH,)),
+            dma((6,)),
+        ],
+        compiler_params=pltpu.CompilerParams(
+            collective_id=0, has_side_effects=True, vmem_limit_bytes=58 * 2**20
+        ),
+        cost_estimate=pl.CostEstimate(flops=4 * 10**9, bytes_accessed=3 * 10**7, transcendentals=0),
+    )(*args)
+
+
+class SquareScatter:
+    def __init__(self, place, block, via, final, send, recv, stage=None):
+        self.p, self.block, self.via, self.final = place, block, via, final
+        self.send, self.recv, self.stage = send, recv, stage
+
+    def _copy(self, i):
+        p = self.p
+        chip, half, way, row = (
+            (p.dchip, 0, 0, 0),
+            (p.dchip, 1, 1, 0),
+            (p.xchip, 0, 0, 1),
+            (p.ychip, 1, 1, 2),
+            (p.xchip, 1, 0, 1),
+            (p.ychip, 0, 1, 2),
+        )[i]
+        land = self.via.at[way] if row == 0 else self.final.at[way, half]
+        return rcopy(
+            self.block(chip, half),
+            land,
+            self.send.at[row, half],
+            self.recv.at[row, half],
+            (p.xnbr, p.ynbr)[way],
+        )
+
+    def start(self, *which):
+        for i in which:
+            self._copy(i).start()
+
+    def second(self):
+        p = self.p
+        for way, chip, i in ((1, p.xchip, 4), (0, p.ychip, 5)):
+            self._copy(way).wait_recv()
+            block = self.block(chip, way)
+            if self.stage is None:
+                more = self.via[way]
+            else:
+                fetch = pltpu.make_async_copy(self.via.at[way], *self.stage)
+                fetch.start()
+                fetch.wait()
+                more = self.stage[0][...]
+            block[...] = (block[...].astype(F32) + more.astype(F32)).astype(BF16)
+            self.start(i)
+
+    def arrive(self, way, r):
+        here = self.final.at[way, r]
+        rcopy(
+            here, here, self.send.at[1 + way, r], self.recv.at[1 + way, r], self.p.xnbr
+        ).wait_recv()
+
+    def drain(self):
+        for i in range(6):
+            self._copy(i).wait_send()
+
+
+def norm_back(rows, grad, gain):
+    root = inverse_root(rows)
+    u = grad * gain
+    back = root * u - rows * (root * root * root * jnp.mean(u * rows, -1, keepdims=True))
+    return back, jnp.sum(grad * rows * root, 0, keepdims=True)
+
+
+def backward_kernel(
+    big, proj, rows_in, heads_q, pair, mixed, middle, rows_mid, rows_grad,
+    tokens, grad_out, attn_gain, mlp_gain, cosine, sine,
+    out, grad_in, g_gate, g_up, g_down, g_query, g_out, g_pair, sums, final, via, sib_land,
+    vbig, hid, d_g, d_u, part, part_o, land, land_o, near_at, back, probs_at, d_s_at, d_mixed, d_lin, d_pair, pair_land,
+    swap_land, d_middle, total, stage, result,
+    gp, gp_land, gp_via_q, gp_fin_q, gp_via_o, gp_fin_o, pair_z, vec, vec_land,
+    load_sem, s_send, s_recv, z_send, z_recv, near_send, near_recv, sq_send, sq_recv, sib_send, sib_recv,
+    gp_send, gp_recv, misc_send, misc_recv, v_send, v_recv, stage_sem, out_sem, near_free,
+):
+    p = Place(4)
+    z, core = p.z, p.core
+    other = 1 - core
+    unit = tokens.shape[0] // NCH
+    wide = unit * p.depth
+    d_model = tokens.shape[1]
+    shard = d_model // 8
+    q_width = mixed.shape[1]
+    heads = q_width // HD
+    scale = 1.0 / math.sqrt(HD)
+
+    loads = [pltpu.make_async_copy(big.at[k], vbig.at[k], load_sem.at[k]) for k in range(3)]
+    for copy in loads:
+        copy.start()
+    p.greet(False)
+    for copy in loads:
+        copy.wait()
+
+    def rows_of(ref, ch, s):
+        return ref.at[pl.ds(pl.multiple_of(ch * wide + s * unit, unit), unit), :]
+
+    scatter_a = LineScatter(p, lambda ch, s: rows_of(part, ch, s), land, s_send.at[0], s_recv.at[0])
+    scatter_o = LineScatter(
+        p, lambda ch, s: rows_of(part_o, ch, s), land_o, s_send.at[1], s_recv.at[1]
+    )
+    scatter_i = LineScatter(p, lambda ch, s: rows_of(part, ch, s), land, s_send.at[2], s_recv.at[2])
+    gather_back = LineGather(p, lambda ch, s: rows_of(back, ch, s), z_send, z_recv)
+
+    def near(k, ch):
+        return rcopy(
+            near_at.at[0, ch], near_at.at[1, ch], near_send.at[k, ch], near_recv.at[k, ch], p.sib
+        )
+
+    def hidden(slot, ch):
+        rows = pl.ds(ch * wide, wide)
+        a2 = rows_mid[slot, rows, :]
+        go = rows_grad[slot, rows, :]
+        for first in range(0, HALF, 256):
+            cols = slice(first, min(first + 256, HALF))
+            gate = dot(a2, vbig[0, :, cols])
+            up = dot(a2, vbig[1, :, cols])
+            d_m = dot(go, vbig[2, :, cols])
+            sg = 1.0 / (1.0 + jnp.exp(-gate))
+            silu = gate * sg
+            hid[slot, rows, cols] = (silu * up).astype(BF16)
+            d_g[slot, rows, cols] = (d_m * up * sg * (1.0 + gate * (1.0 - sg))).astype(BF16)
+            d_u[slot, rows, cols] = (d_m * silu).astype(BF16)
+
+    def d_mid_rows(slot, ch):
+        rows = pl.ds(ch * wide, wide)
+        return dot(d_g[slot, rows, :], vbig[0], 1, 1) + dot(d_u[slot, rows, :], vbig[1], 1, 1)
+
+    for ch in range(NCH):
+        hidden(other, ch)
+        near_at[0, ch] = d_mid_rows(other, ch).astype(BF16)
+        near(0, ch).start()
+    for ch in range(NCH):
+        hidden(core, ch)
+        term = d_mid_rows(core, ch)
+        near(0, ch).wait_recv()
+        part[ch * wide : (ch + 1) * wide, :] = (term + near_at[1, ch].astype(F32)).astype(BF16)
+        scatter_a.step(ch, 3)
+    pl.semaphore_signal(near_free, inc=1, device_id=p.sib, device_id_type=MESH)
+
+    for ch in range(NCH):
+        rows = pl.ds(ch * wide, wide)
+        near(0, ch).wait_send()
+        near_at[0, ch] = dot(hid[other, rows, :], vbig[2], 1, 1).astype(BF16)
+        if ch == 0:
+            pl.semaphore_wait(near_free, 1)
+        near(1, ch).start()
+    for ch in range(NCH):
+        scatter_a.step(ch, 2)
+    for ch in range(NCH):
+        rows = pl.ds(ch * wide, wide)
+        term = dot(hid[core, rows, :], vbig[2], 1, 1)
+        near(1, ch).wait_recv()
+        part_o[ch * wide : (ch + 1) * wide, :] = (term + near_at[1, ch].astype(F32)).astype(BF16)
+    for ch in range(NCH):
+        scatter_a.step(ch, 1)
+
+    squares = [
+        SquareScatter(
+            p,
+            lambda chip, r, k=k: vbig.at[
+                k, pl.ds(pl.multiple_of((chip * 2 + r) * shard, 16), shard), :
+            ],
+            via.at[k],
+            final.at[k],
+            sq_send.at[k],
+            sq_recv.at[k],
+            (stage.at[0], stage_sem.at[0]),
+        )
+        for k in range(3)
+    ]
+
+    def weight_grad(k, chip):
+        wide_cols = pl.ds(pl.multiple_of(chip * 2 * shard, HD), 2 * shard)
+        left = rows_grad if k == 2 else rows_mid
+        right = (d_g, d_u, hid)[k]
+        term = dot(left[0, :, wide_cols], right[0], 0, 0) + dot(left[1, :, wide_cols], right[1], 0, 0)
+        vbig[k, pl.ds(pl.multiple_of(chip * 2 * shard, 16), 2 * shard), :] = term.astype(BF16)
+
+    def weight_grads(k):
+        weight_grad(k, p.dchip)
+        squares[k].start(0, 1)
+        weight_grad(k, p.xchip)
+        squares[k].start(2)
+        weight_grad(k, p.ychip)
+        squares[k].start(3)
+        weight_grad(k, p.chip)
+
+    weight_grads(0)
+    gain_sum = jnp.zeros((1, d_model), F32)
+    for ch in range(NCH):
+        half = slice(ch * unit, (ch + 1) * unit)
+        scatter_a.total(ch, total)
+        grad, gain_part = norm_back(middle[half, :], total[...], mlp_gain[...])
+        gain_sum = gain_sum + gain_part
+        d_mid = grad_out[half, :].astype(F32) + grad
+        d_middle[half, :] = d_mid
+        back[pl.ds(pl.multiple_of(ch * wide + z * unit, unit), unit), :] = d_mid.astype(BF16)
+        gather_back.own(ch)
+    scatter_a.drain()
+    for ch in range(NCH):
+        scatter_o.step(ch, 3)
+    weight_grads(1)
+    for ch in range(NCH):
+        gather_back.step(ch, 1)
+        scatter_o.step(ch, 2)
+    weight_grads(2)
+    squares[0].second()
+    for ch in range(NCH):
+        gather_back.step(ch, 2)
+        scatter_o.step(ch, 1)
+    squares[1].second()
+    for ch in range(NCH):
+        gather_back.step(ch, 3)
+
+    fetch_in = [
+        pltpu.make_async_copy(
+            rows_in.at[pl.ds(ch * wide, wide), :], near_at.at[0, ch], load_sem.at[3 + ch]
+        )
+        for ch in range(NCH)
+    ]
+    for ch in range(NCH):
+        near(1, ch).wait_send()
+        fetch_in[ch].start()
+    d_pair[...] = jnp.zeros(d_pair.shape, F32)
+    for ch in range(NCH):
+        rows = pl.ds(ch * wide, wide)
+        d_mixed[rows, :] = dot(back[rows, :], proj[:, q_width + 2 * HD :]).astype(BF16)
+
+        def one_head(h):
+            cols = slice(h * HD, (h + 1) * HD)
+            keep = allowed(core, ch, unit, p.depth, wide)
+            queries = heads_q[h, rows, :]
+            probs, pb = softmax(queries, pair, keep)
+            d_o = d_mixed[rows, cols]
+            d_p = dot(d_o, both(pair, HD), 1, 1)
+            d_s_at[...] = (probs * (d_p - jnp.sum(probs * d_p, -1, keepdims=True))).astype(BF16)
+            probs_at[...] = pb
+            keys = NCH * wide
+            d_q = dot(d_s_at[...], both(pair, 0)) * scale
+            d_lin[rows, cols] = turn(d_q, cosine[rows, :], -sine[rows, :]).astype(BF16)
+            for slot in (0, 1):
+                span = slice(slot * keys, (slot + 1) * keys)
+                d_pair[slot, :, 0:HD] += dot(d_s_at[:, span], queries, 0, 0) * scale
+                d_pair[slot, :, HD:] += dot(probs_at[:, span], d_o, 0, 0)
+
+        for h in range(heads):
+            one_head(h)
+
+    pair_land[0] = d_pair[other].astype(BF16)
+    across = rcopy(
+        pair_land.at[0], pair_land.at[1], misc_send.at[0], misc_recv.at[0], p.sib
+    )
+    across.start()
+    gp_out = q_width + HD
+    for chip in range(4):
+        wide_cols = slice(chip * 2 * shard, (chip + 1) * 2 * shard)
+        gp[wide_cols, gp_out:] = dot(back[:, wide_cols], mixed[...], 0, 0).astype(BF16)
+    across.wait_recv()
+    d_pair[core] += pair_land[1].astype(F32)
+    which = lax.rem(z, 2)
+    mine = pl.ds(pl.multiple_of(which * HD, HD), HD)
+    theirs = pl.ds(pl.multiple_of((1 - which) * HD, HD), HD)
+    swap_land[0] = d_pair[core, :, theirs].astype(BF16)
+    swap = rcopy(
+        swap_land.at[0],
+        swap_land.at[1],
+        misc_send.at[1],
+        misc_recv.at[1],
+        (p.dp, z + 1 - 2 * which),
+    )
+    swap.start()
+    squares[2].second()
+    swap.wait_recv()
+    own = d_pair[core, :, mine] + swap_land[1].astype(F32)
+    is_key = which == 0
+    own = own * jnp.where(is_key, cosine[...], 1.0) - pltpu.roll(own, HD // 2, 1) * jnp.where(
+        is_key, sine[...], 0.0
+    )
+    d_lin[:, q_width:] = own.astype(BF16)
+
+    w_mine = proj[:, pl.ds(pl.multiple_of(q_width + which * HD, HD), HD)]
+    for ch in range(NCH):
+        rows = slice(ch * wide, (ch + 1) * wide)
+        part[rows, :] = (
+            dot(d_lin[rows, :q_width], proj[:, :q_width], 1, 1) + dot(d_lin[rows, q_width:], w_mine, 1, 1)
+        ).astype(BF16)
+        scatter_i.step(ch, 3)
+    for copy in fetch_in:
+        copy.wait()
+    for chip in range(4):
+        wide_cols = slice(chip * 2 * shard, (chip + 1) * 2 * shard)
+        gp[wide_cols, :gp_out] = (
+            dot(near_at[0, 0, :, wide_cols], d_lin[:wide, :], 0, 0)
+            + dot(near_at[0, 1, :, wide_cols], d_lin[wide:, :], 0, 0)
+        ).astype(BF16)
+
+    def gp_near(chip):
+        src = gp.at[pl.ds(pl.multiple_of((chip * 2 + other) * shard, 16), shard), :]
+        return rcopy(src, gp_land.at[chip], misc_send.at[2 + chip], misc_recv.at[2 + chip], p.sib)
+
+    for chip in range(4):
+        gp_near(chip).start()
+    for ch in range(NCH):
+        scatter_i.step(ch, 2)
+
+    def gp_rows(chip):
+        return pl.ds(pl.multiple_of((chip * 2 + core) * shard, 16), shard)
+
+    for chip in range(4):
+        gp_near(chip).wait_recv()
+        gp[gp_rows(chip), :] = (
+            gp[gp_rows(chip), :].astype(F32) + gp_land[chip].astype(F32)
+        ).astype(BF16)
+    half_rows = shard // 2
+    gp_squares = [
+        SquareScatter(
+            p,
+            lambda chip, r, cols=cols: gp.at[
+                pl.ds(pl.multiple_of((chip * 2 + core) * shard + r * half_rows, 16), half_rows),
+                cols,
+            ],
+            gvia,
+            gfin,
+            gp_send.at[i],
+            gp_recv.at[i],
+        )
+        for i, (cols, gvia, gfin) in enumerate(
+            ((slice(0, gp_out), gp_via_q, gp_fin_q), (slice(gp_out, gp_out + q_width), gp_via_o, gp_fin_o))
+        )
+    ]
+    for square in gp_squares:
+        square.start(0, 1, 2, 3)
+    for ch in range(NCH):
+        scatter_i.step(ch, 1)
+    for ch in range(NCH):
+        half = slice(ch * unit, (ch + 1) * unit)
+        scatter_o.total(ch, total)
+        out[half, :] = middle[half, :] + total[...]
+    for square in gp_squares:
+        square.second()
+
+    def kept(k, r):
+        for way in (0, 1):
+            squares[k].arrive(way, r)
+        fetch = [
+            pltpu.make_async_copy(final.at[k, way, r], stage.at[way], stage_sem.at[way])
+            for way in (0, 1)
+        ]
+        for copy in fetch:
+            copy.start()
+        for copy in fetch:
+            copy.wait()
+        block = big_block(k, r)[...]
+        return block.astype(F32) + stage[0].astype(F32) + stage[1].astype(F32)
+
+    def big_block(k, r):
+        return vbig.at[k, pl.ds(pl.multiple_of((p.chip * 2 + r) * shard, 16), shard), :]
+
+    def sib_copy(k):
+        return rcopy(big_block(k, other), sib_land.at[k], sib_send.at[k], sib_recv.at[k], p.sib)
+
+    def keep_big(k):
+        big_block(k, other)[...] = kept(k, other).astype(BF16)
+        sib_copy(k).start()
+
+    def result_copy(k):
+        return pltpu.make_async_copy(result, (g_gate, g_up, g_down)[k], out_sem.at[k])
+
+    def finish_big(k):
+        own = kept(k, core)
+        sib_copy(k).wait_recv()
+        fetch = pltpu.make_async_copy(sib_land.at[k], stage.at[0], stage_sem.at[0])
+        fetch.start()
+        fetch.wait()
+        if k > 0:
+            result_copy(k - 1).wait()
+        theirs = stage[0].astype(F32)
+        cols = result.shape[1]
+        for c in (0, 1):
+
+            @pl.when(core == c)
+            def _(c=c):
+                result[:, :HALF] = own if c == 0 else theirs
+                result[:, HALF:] = (theirs if c == 0 else own)[:, : cols - HALF]
+
+        result_copy(k).start()
+
+    keep_big(0)
+    in_gain = jnp.zeros((1, d_model), F32)
+    for ch in range(NCH):
+        half = slice(ch * unit, (ch + 1) * unit)
+        scatter_i.total(ch, total)
+        grad, gain_part = norm_back(tokens[half, :].astype(F32), total[...], attn_gain[...])
+        in_gain = in_gain + gain_part
+        grad_in[half, :] = d_middle[half, :] + grad
+
+    vec[...] = jnp.zeros(vec.shape, F32)
+    bias = jnp.sum(d_lin[...].astype(F32), 0, keepdims=True)
+    for i in range(heads):
+        vec[pl.ds(z * heads + i, 1), :] = bias[:, i * HD : (i + 1) * HD]
+    n_q = heads * p.depth
+    vec[pl.ds(n_q + which * 2 + z // 2, 1), :] = bias[:, q_width:]
+    for i in range(d_model // HD):
+        cols = slice(i * HD, (i + 1) * HD)
+        vec[n_q + 4 + i : n_q + 5 + i, :] = in_gain[:, cols]
+        vec[n_q + 4 + d_model // HD + i : n_q + 5 + d_model // HD + i, :] = gain_sum[:, cols]
+    for i, dev in enumerate((p.sib, p.xnbr, p.ynbr)):
+        step = rcopy(vec, vec_land.at[i], v_send.at[i], v_recv.at[i], dev)
+        step.start()
+        step.wait()
+        vec[...] += vec_land[i]
+
+    def z_other(d):
+        return lax.rem(z + d, p.depth)
+
+    keep_big(1)
+    keep_big(2)
+    for i, square in enumerate(gp_squares):
+        for r in (0, 1):
+            square.arrive(0, r)
+            square.arrive(1, r)
+            cols, fin = ((slice(0, gp_out), gp_fin_q), (slice(gp_out, gp_out + q_width), gp_fin_o))[i]
+            block = gp[
+                pl.ds(pl.multiple_of((p.chip * 2 + core) * shard + r * half_rows, 16), half_rows), cols
+            ]
+            value = block.astype(F32) + fin[0, r].astype(F32) + fin[1, r].astype(F32)
+            rows = slice(r * half_rows, (r + 1) * half_rows)
+            if i == 0:
+                g_query[rows, :] = value[:, :q_width]
+                pair_z[0, rows, :] = value[:, q_width:]
+            else:
+                g_out[rows, :] = value
+
+    quarter = shard // p.depth
+    g_pair[z] = pair_z[0, pl.ds(pl.multiple_of(z * quarter, 8), quarter), :]
+
+    def along(d):
+        dev = (p.dp, z_other(d))
+        return (
+            rcopy(
+                pair_z.at[0, pl.ds(pl.multiple_of(z_other(d) * quarter, 8), quarter), :],
+                pair_z.at[1, pl.ds((d - 1) * quarter, quarter), :],
+                v_send.at[2 + d],
+                v_recv.at[2 + d],
+                dev,
+            ),
+            rcopy(vec, vec_land.at[2 + d], v_send.at[5 + d], v_recv.at[5 + d], dev),
+        )
+
+    for d in (1, 2, 3):
+        for copy in along(d):
+            copy.start()
+    for k in range(3):
+        finish_big(k)
+    for d in (1, 2, 3):
+        for copy in along(d):
+            copy.wait()
+        g_pair[lax.rem(z + p.depth - d, p.depth)] = pair_z[1, (d - 1) * quarter : d * quarter, :]
+    sums[...] = vec[...] + vec_land[3] + vec_land[4] + vec_land[5]
+
+    for line in (scatter_o, scatter_i, gather_back):
+        line.drain()
+    for square in squares + gp_squares:
+        square.drain()
+    across.wait_send()
+    swap.wait_send()
+    for chip in range(4):
+        gp_near(chip).wait_send()
+    for k in range(3):
+        sib_copy(k).wait_send()
+    result_copy(2).wait()
+
+
+def backward_call(depth, args, cols):
+    big, proj, rows_in, heads_q, pair, mixed, middle = args[:7]
+    rows, d_model = middle.shape
+    q_width = mixed.shape[1]
+    total_rows = rows * depth
+    unit = rows // NCH
+    wide = unit * depth
+    shard = d_model // 8
+    vm = pl.BlockSpec(memory_space=pltpu.VMEM)
+    anyspace = pl.BlockSpec(memory_space=pl.ANY)
+    sds = jax.ShapeDtypeStruct
+    dma = pltpu.SemaphoreType.DMA
+    n_sum = 2 * d_model // HD + d_model // HD + 4
+    n_sum = -(-n_sum // 8) * 8
+    gp_cols = q_width + HD + q_width
+    half_rows = shard // 2
+    out_shape = (
+        sds((rows, d_model), F32),
+        sds((rows, d_model), F32),
+        sds((shard, cols), F32),
+        sds((shard, cols), F32),
+        sds((shard, cols), F32),
+        sds((shard, q_width), F32),
+        sds((shard, q_width), F32),
+        sds((depth, shard // depth, HD), F32),
+        sds((n_sum, HD), F32),
+        sds((3, 2, 2, shard, HALF), BF16),
+        sds((3, 2, shard, HALF), BF16),
+        sds((3, shard, HALF), BF16),
+    )
+    v = pltpu.VMEM
+    return pl.pallas_call(
+        backward_kernel,
+        out_shape=out_shape,
+        in_specs=[anyspace, vm, anyspace] + [vm] * (len(args) - 3),
+        out_specs=(vm, vm, anyspace, anyspace, anyspace, vm, vm, vm, vm, anyspace, anyspace, anyspace),
+        scratch_shapes=[
+            v((3, d_model, HALF), BF16),
+            v((2, total_rows, HALF), BF16),
+            v((2, total_rows, HALF), BF16),
+            v((2, total_rows, HALF), BF16),
+            v((total_rows, d_model), BF16),
+            v((total_rows, d_model), BF16),
+            v((2, NCH, depth - 1, unit, d_model), BF16),
+            v((2, NCH, depth - 1, unit, d_model), BF16),
+            v((2, NCH, wide, d_model), BF16),
+            v((total_rows, d_model), BF16),
+            v((wide, 2 * total_rows), BF16),
+            v((wide, 2 * total_rows), BF16),
+            v((total_rows, q_width), BF16),
+            v((total_rows, q_width + HD), BF16),
+            v((2, total_rows, 2 * HD), F32),
+            v((2, total_rows, 2 * HD), BF16),
+            v((2, total_rows, HD), BF16),
+            v((rows, d_model), F32),
+            v((unit, d_model), F32),
+            v((2, shard, HALF), BF16),
+            v((shard, cols), F32),
+            v((d_model, gp_cols), BF16),
+            v((4, shard, gp_cols), BF16),
+            v((2, half_rows, q_width + HD), BF16),
+            v((2, 2, half_rows, q_width + HD), BF16),
+            v((2, half_rows, q_width), BF16),
+            v((2, 2, half_rows, q_width), BF16),
+            v((2, shard, HD), F32),
+            v((n_sum, HD), F32),
+            v((6, n_sum, HD), F32),
+            dma((3 + NCH,)),
+            dma((3, 2, NCH, depth)),
+            dma((3, 2, NCH, depth)),
+            dma((2, NCH, depth)),
+            dma((2, NCH, depth)),
+            dma((2, NCH)),
+            dma((2, NCH)),
+            dma((3, 3, 2)),
+            dma((3, 3, 2)),
+            dma((3,)),
+            dma((3,)),
+            dma((2, 3, 2)),
+            dma((2, 3, 2)),
+            dma((6,)),
+            dma((6,)),
+            dma((9,)),
+            dma((9,)),
+            dma((2,)),
+            dma((3,)),
+            pltpu.SemaphoreType.REGULAR,
+        ],
+        compiler_params=pltpu.CompilerParams(
+            collective_id=1, has_side_effects=True, vmem_limit_bytes=62 * 2**20
+        ),
+        cost_estimate=pl.CostEstimate(flops=4 * 10**10, bytes_accessed=5 * 10**7, transcendentals=0),
+    )(*args)
+
+
+def chunk_order(rows, depth):
+    unit = rows.shape[0] // (depth * NCH)
+    return rows.reshape(depth, NCH, unit, *rows.shape[1:]).swapaxes(0, 1).reshape(rows.shape)
+
+
+def paired_shards(
+    tokens, grad_out, attn_gain, w_query, b_query, w_key, b_key, w_value, b_value, w_out, mlp_gain, w_gate, w_up, w_down
+):
+    depth = lax.axis_size("tensor")
+    rows = tokens.shape[0] * depth
+    members = lax.axis_size("dp") // GROUPS
+    group_tok = members * rows
+    position, _ = layout(lax.axis_index("dp") * rows, rows, group_tok, group_tok // 2)
+    cosine, sine = tables(chunk_order(position, depth), HD)
+    half = HD // 2
+    sine = jnp.concatenate([-sine[:, :half], sine[:, half:]], 1)
+    gains = (attn_gain[None], mlp_gain[None])
+    biases = (b_query[None], b_key[None], b_value[None])
+    kept = forward_call(
+        depth,
+        (tokens, grad_out, *gains, w_query, w_key, w_value, w_out, w_gate, w_up, w_down, *biases, cosine, sine),
+    )
+    got = backward_call(depth, (*kept, tokens, grad_out, *gains, cosine, sine), w_gate.shape[1])
+    out, grad_in, g_gate, g_up, g_down, g_query, g_out, g_pair, sums = got[:9]
+    flat = sums.reshape(-1)
+    place = lax.axis_index("dp") * depth + lax.axis_index("tensor")
+    count = lax.axis_size("dp") * depth
+    parts, first = [], 0
+    for size in (b_query.shape[0], b_key.shape[0], b_value.shape[0], attn_gain.shape[0], mlp_gain.shape[0]):
+        parts.append(lax.dynamic_slice_in_dim(flat, first + place * (size // count), size // count))
+        first += size
+    g_key = jnp.concatenate([g_pair[0], g_pair[2]], 1)
+    g_value = jnp.concatenate([g_pair[1], g_pair[3]], 1)
+    return (
+        out, grad_in, parts[3], g_query, parts[0], g_key, parts[1], g_value, parts[2], g_out, parts[4], g_gate, g_up, g_down
+    )
+
+
 def solution(mesh):
+    paired = mesh.shape["dp"] == 2 * GROUPS and mesh.shape["tensor"] == 4
     return jax.shard_map(
-        shards,
+        paired_shards if paired else shards,
         mesh=mesh,
         in_specs=(
             P(("dp", "tensor"), None),

time: 1080 us -> 326 us (0.30)
  waiting for transfers between devices: 800 us -> 0 us
  Pallas kernels: 0 us -> 299 us
  matrix products: 111 us -> 0 us
  blocking collectives: 54.3 us -> 0 us
  other arithmetic: 34.7 us -> 3.27 us
  starting transfers between devices: 19.8 us -> 0 us
  local copies, waits for them, and re-layouts: 30.1 us -> 15.4 us
  between operations: 15.5 us -> 1.18 us
    reduce_scatter x10 -> x0, waiting for transfers between devices: 441 us -> none  [the longest x1 103 us: shards(): lax.psum_scatter(pair_grad[:, key_width:], ('dp', 'tensor'), scatter_dime...]
    pallas_call x0 -> x2, Pallas kernels: none -> 299 us  [the longest x1 171 us: backward_call(): pl.pallas_call(backward_kernel, out_shape=out_shape, in_specs=[anyspace,...]
    all_gather x9 -> x0, waiting for transfers between devices: 293 us -> none  [the longest x1 50.7 us: shards(): lax.all_gather(w_down, 'dp', axis=0, tiled=True)]
    dot_general x24 -> x0, matrix products: 111 us -> none  [the longest x1 13.4 us: shards(): d_hidden = jnp.dot(rows_grad, back_down, preferred_element_type=jnp.float32)]
    unnamed x21 -> x0, waiting for transfers between devices: 60.5 us -> none
    unnamed x1 -> x0, blocking collectives: 43.9 us -> none
    ppermute x4 -> x0, starting transfers between devices: 18.1 us -> none  [the longest x3 16.4 us: from_behind(): return lax.ppermute(x, axis, pairs)]
    convert_element_type x10 -> x0, other arithmetic: 16.4 us -> none  [the longest x4 8.26 us: reduce_weights(): return (lax.psum_scatter(terms[0].astype(jnp.bfloat16), 'dp', scatter_dim...]
  transfers between devices with their start and end apart: 24 -> 0, of which waited for: 19 -> 0; matrix products, arithmetic and copies ran while one was open for 12% -> 0% of each run, Pallas kernels for 0% -> 0%
where the time goes in v1:
time: 326 us; the launch traced here: 319 us
  Pallas kernels  299 us (92%)
  local copies, waits for them, and re-layouts  15.4 us (5%)
  other arithmetic  3.27 us (1%)
    pallas_call x1, Pallas kernels, backward_call(): pl.pallas_call(backward_kernel, out_shape=out_shape, in_specs=[anyspace,...  171 us
    pallas_call x1, Pallas kernels, forward_call(): pl.pallas_call(forward_kernel, out_shape=out_shape, in_specs=[vm] * len(a...  128 us
    unnamed x25, local copies, waits for them, and re-layouts  9.98 us

profile of v1, /device:TPU:10, one launch (start us, length us, event | category | flops | bytes accessed | tf_op | source)
XLA Modules:
  0.0 319.1 jit_solution(11436618525843441663)
XLA Ops:
  0.6 0.0 copy-start.6
  0.7 0.0 copy-start.7
  0.7 0.0 copy-start.8
  0.7 0.1 add.88
  0.8 1.0 fusion
  1.8 1.0 pad_maximum_fusion
  2.8 0.0 copy-done.6
  2.8 0.6 broadcast_in_dim.17.attn_gain
  3.4 0.0 copy-done.7
  3.4 0.6 broadcast_in_dim.18.mlp_gain
  4.0 0.0 copy-done.8
  4.0 0.6 broadcast_in_dim.19.b_query
  4.6 128.0 %shard_map.245 = (bf16[3,1536,1152]{2,1,0:T(8,128)(2,1)}, bf16[1536,1024]{1,0:T(8,128)(2,1)}, bf16[512,1536]{1,0:T(8,128)(2,1)}, bf16[3,512,128]{2,1,0:T(8,128)(...) custom-call(bf16[128,1536]{1,0:T(8,128)(2,1)} %tokens.3, ...), custom_call_target="tpu_custom_call" | custom-call | flops 4000000000 | bytes 30000000 | tf_op jit(solution)/shard_map/pallas_call | solution.py:861
  132.6 171.2 %shard_map.246 = (f32[128,1536]{1,0:T(8,128)}, f32[128,1536]{1,0:T(8,128)}, f32[192,2240]{1,0:T(8,128)}, f32[192,2240]{1,0:T(8,128)}, f32[192,2240]{1,0:T(8,128)...) custom-call(bf16[3,1536,1152]{2,1,0:T(8,128)(2,1)} %get-tuple-elemen, ...), custom_call_target="tpu_custom_call" | custom-call | flops 40000000000 | bytes 50000000 | tf_op jit(solution)/shard_map/pallas_call | solution.py:1397
  303.8 0.0 copy-start.3
  303.8 0.0 copy-start.5
  303.8 0.9 slice_bitcast_fusion.1
  304.7 0.6 pad_maximum_fusion.3
  305.3 0.6 pad_maximum_fusion.2
  305.9 1.4 fusion.5
  307.3 1.3 fusion.6
  308.6 0.0 copy-start.4
  308.6 0.0 copy-start.2
  308.6 2.2 copy.35
  310.9 0.0 copy-done.3
  310.9 0.9 copy.36
  311.7 0.0 copy-done.5
  311.7 0.7 copy.37
  312.5 0.0 copy-done.4
  312.5 0.7 copy.38
  313.2 0.0 copy-done.2
  313.2 0.0 copy-start.1
  313.2 1.2 copy.39
  314.4 0.9 copy-done.1
  315.3 0.0 copy-start
  315.3 1.2 copy.40
  316.5 0.9 copy-done
  317.4 1.2 copy.41
  (3 shorter events, 0.0 us)
Async XLA Ops:
  0.6 2.2 copy-start.6
  0.7 2.8 copy-start.7
  0.7 3.3 %copy-start.8 = (f32[1536]{0:T(1024)S(1)}, f32[1536]{0:T(1024)}, u32[]{:S(2)}) copy-start(f32[1536]{0:T(1024)} %param.18) | copy-start | bytes 18436
  303.8 7.1 %copy-start.3 = (f32[128,1536]{1,0:T(8,128)S(1)}, f32[128,1536]{1,0:T(8,128)}, u32[]{:S(2)}) copy-start(f32[128,1536]{1,0:T(8,128)} %get-tuple-element.79) | copy-start | bytes 2359300
  303.8 7.9 %copy-start.5 = (f32[192,384]{1,0:T(8,128)S(1)}, f32[192,384]{1,0:T(8,128)}, u32[]{:S(2)}) copy-start(f32[192,384]{1,0:T(8,128)} %get-tuple-element.81) | copy-start | bytes 884740
  308.6 3.8 %copy-start.4 = (f32[192,384]{1,0:T(8,128)S(1)}, f32[192,384]{1,0:T(8,128)}, u32[]{:S(2)}) copy-start(f32[192,384]{1,0:T(8,128)} %get-tuple-element.87) | copy-start | bytes 884740
  308.6 4.5 %copy-start.2 = (f32[192,2240]{1,0:T(8,128)S(1)}, f32[192,2240]{1,0:T(8,128)}, u32[]{:S(2)}) copy-start(f32[192,2240]{1,0:T(8,128)} %get-tuple-element.89) | copy-start | bytes 5160964
  313.2 2.1 copy-start.1
  315.3 2.1 copy-start
